TPU v7x, 128 devices: a whole 4x4x4 slice. The times are simulated.
128 devices in a mesh: rep: 8 (over y, core), head: 16 (over z, x).
Axes of the slice: x: 4, y: 4, z: 4, core: 2. Of those that a mesh axis runs over, the one named last changes fastest.
Arguments:
- prefill_states: bfloat16 [256, 2, 128, 64, 128], P('rep', None, 'head'), may hold values from -6 to 6
- inner_tail: bfloat16 [256, 2, 3, 8192], P('rep', None, None, 'head'), may hold values from -6 to 6
- group_tail: bfloat16 [256, 2, 3, 2048], P('rep'), may hold values from -6 to 6
- assignment: int32 [256, 1], P('rep'), may hold values from 0 to 31; in each aligned block of 32 rows (0 to 31, 32 to 63, ...) at most 2 rows name the same one
- decode_inner: bfloat16 [8, 16, 8, 2, 2, 2, 2048], P('rep', 'head'), may hold values from -6 to 6
- decode_groups: bfloat16 [8, 4, 8, 2, 2, 2, 2048], P('rep'), may hold values from -6 to 6
- decode_rate: bfloat16 [8, 16, 8, 2, 2, 2, 32], P('rep', 'head'), may hold values from -3 to 3
- conv_inner: float32 [2, 4, 8192], replicated, may hold values from -3 to 3
- conv_group: float32 [2, 4, 2048], replicated, may hold values from -3 to 3
- bias_inner: float32 [2, 8192], replicated, may hold values from -3 to 3
- bias_group: float32 [2, 2048], replicated, may hold values from -3 to 3
- rate_bias: float32 [2, 128], replicated, may hold values from -4 to -1
- decay_log: float32 [2, 128], replicated, may hold values from 0 to 2.8
- skip_gain: float32 [2, 128], replicated, may hold values from 0.5 to 2
Outputs:
- decoded: bfloat16 [8, 16, 8, 2, 2, 2, 2048], P('rep', 'head')
Inputs may be any that keep to these rules, and one draw needn't show every extreme that they name: `assignment`: the 32 requests of one index of rep name any one replica at most 2 times, a bound that some block reaches.
All inputs are finite; a program needn't handle non-finite values.
Results may differ from a plain program's by a relative error of at most 0.001.
Values may be sent and summed in bfloat16 or wider, within the bound.
No kernel may reach another device: no remote copies, remote signals or barrier semaphores. Data moves between devices by JAX's collectives and lax.ppermute only.
A program may use at most 128 MiB of HBM per device.

v0:
```python
import jax
import jax.numpy as jnp
from jax import lax
from jax.sharding import PartitionSpec as P

GROUPS = 8
TP = 4


def conv_update(history, fresh, weight, offset):
    window = jnp.concatenate([history, fresh[..., None, :]], axis=-2)
    summed = jnp.sum(weight * window.astype(jnp.float32), axis=-2) + offset
    return (jax.nn.silu(summed), window[..., 1:, :])


def state_step(
    states, inner_act, write_vec, read_vec, rate_raw, rate_shift, damping_log, skip_part
):
    step_size = jax.nn.softplus(rate_raw.astype(jnp.float32) + rate_shift)
    damping = jnp.exp(-step_size * jnp.exp(damping_log))
    states = (
        damping[..., None, None] * states
        + (step_size[..., None] * inner_act)[..., None] * write_vec[..., None, None, :]
    )
    output = (
        jnp.einsum("...upn,...n->...up", states, read_vec, precision=lax.Precision.HIGHEST)
        + skip_part[..., None] * inner_act
    )
    return (states, output)


def spread_groups(vector, repeat_count):
    shaped = vector.reshape(vector.shape[:-1] + (GROUPS, -1))
    return jnp.repeat(shaped, repeat_count, axis=-2)


def rank_slice(table, head_count, rank_idx):
    shaped = table.reshape(table.shape[:-1] + (head_count, TP, -1))
    return lax.dynamic_index_in_dim(shaped, rank_idx, axis=shaped.ndim - 2, keepdims=False)


def shards(
    prefill_states,
    inner_tail,
    group_tail,
    assignment,
    decode_inner,
    decode_groups,
    decode_rate,
    conv_inner,
    conv_group,
    bias_inner,
    bias_group,
    rate_bias,
    decay_log,
    skip_gain,
):
    rep_count = lax.axis_size("rep")
    head_count = lax.axis_size("head")
    sub_count = head_count // TP
    head_pos = lax.axis_index("head")
    sub_idx = head_pos // TP
    rank_idx = head_pos % TP
    req_local, layer_count, heads_local, head_width, state_width = prefill_states.shape
    heads_rank = heads_local // TP
    rank_width = heads_rank * head_width
    hist_len = inner_tail.shape[2]
    slot_cap = decode_inner.shape[3]
    step_count = decode_inner.shape[5]
    group_width = group_tail.shape[3]
    piece = group_width // head_count
    group_span = group_width // 2
    zero_half = jnp.zeros((), jnp.bfloat16)
    chosen = assignment[:, 0]
    order = jnp.arange(req_local, dtype=jnp.int32)
    same = chosen[:, None] == chosen[None, :]
    rank_in = jnp.sum((same & (order[None, :] < order[:, None])).astype(jnp.int32), axis=1)
    targets = jnp.arange(rep_count * sub_count, dtype=jnp.int32)
    match = (chosen[None, None, :] == targets[:, None, None]) & (
        rank_in[None, None, :] == jnp.arange(slot_cap, dtype=jnp.int32)[None, :, None]
    )
    present = jnp.any(match, axis=2).reshape(rep_count, sub_count, 1, slot_cap)
    source = jnp.sum(match.astype(jnp.int32) * order[None, None, :], axis=2).reshape(
        rep_count, sub_count, 1, slot_cap
    )
    rank_axis = jnp.arange(TP, dtype=jnp.int32)[None, None, :, None]
    per_layer = []
    for layer_idx in range(layer_count):
        local_states = prefill_states[:, layer_idx].reshape(req_local, TP, rank_width, state_width)
        packed_states = jnp.where(
            present[..., None, None], local_states[source, rank_axis], zero_half
        )
        packed_states = packed_states.reshape(
            rep_count, head_count, slot_cap, rank_width, state_width
        )
        local_inner = (
            inner_tail[:, layer_idx]
            .reshape(req_local, hist_len, TP, rank_width)
            .transpose(0, 2, 1, 3)
        )
        inner_part = local_inner[source, rank_axis]
        local_group = lax.dynamic_slice_in_dim(group_tail[:, layer_idx], head_pos * piece, piece, 2)
        group_part = jnp.broadcast_to(local_group[source], inner_part.shape[:-1] + (piece,))
        packed_tail = jnp.where(
            present[..., None, None], jnp.concatenate([inner_part, group_part], axis=-1), zero_half
        )
        packed_tail = packed_tail.reshape(
            rep_count, head_count, slot_cap, hist_len, rank_width + piece
        )
        got_states, got_tail = (
            lax.all_to_all(
                lax.all_to_all(packed_states, "rep", split_axis=0, concat_axis=0, tiled=True),
                "head",
                split_axis=1,
                concat_axis=1,
                tiled=True,
            ),
            lax.all_to_all(
                lax.all_to_all(packed_tail, "rep", split_axis=0, concat_axis=0, tiled=True),
                "head",
                split_axis=1,
                concat_axis=1,
                tiled=True,
            ),
        )
        states = got_states.astype(jnp.float32).reshape(
            rep_count, head_count, slot_cap, heads_rank, head_width, state_width
        )
        inner_hist = got_tail[..., :rank_width]
        group_hist = (
            got_tail[..., rank_width:]
            .transpose(0, 2, 3, 1, 4)
            .reshape(rep_count, slot_cap, hist_len, group_width)
        )
        weight_inner = rank_slice(conv_inner[layer_idx], head_count, rank_idx).transpose(1, 0, 2)[
            :, None
        ]
        shift_inner = rank_slice(bias_inner[layer_idx], head_count, rank_idx)[:, None]
        rate_shift = rank_slice(rate_bias[layer_idx], head_count, rank_idx)[:, None]
        damping_log = rank_slice(decay_log[layer_idx], head_count, rank_idx)[:, None]
        skip_part = rank_slice(skip_gain[layer_idx], head_count, rank_idx)[:, None]
        fresh_inner = (
            decode_inner[0, 0, :, :, layer_idx]
            .reshape(rep_count, slot_cap, step_count, head_count, rank_width)
            .transpose(0, 3, 1, 2, 4)
        )
        fresh_rate = (
            decode_rate[0, 0, :, :, layer_idx]
            .reshape(rep_count, slot_cap, step_count, head_count, heads_rank)
            .transpose(0, 3, 1, 2, 4)
        )
        fresh_group = lax.dynamic_index_in_dim(decode_groups[0], sub_idx, 0, keepdims=False)[
            :, :, layer_idx
        ]
        outputs = []
        for step_idx in range(step_count):
            inner_act, inner_hist = conv_update(
                inner_hist, fresh_inner[:, :, :, step_idx], weight_inner, shift_inner
            )
            group_act, group_hist = conv_update(
                group_hist,
                fresh_group[:, :, step_idx],
                conv_group[layer_idx],
                bias_group[layer_idx],
            )
            write_vec = spread_groups(group_act[..., :group_span], head_count // GROUPS).transpose(
                0, 2, 1, 3
            )
            read_vec = spread_groups(group_act[..., group_span:], head_count // GROUPS).transpose(
                0, 2, 1, 3
            )
            inner_heads = inner_act.reshape(rep_count, head_count, slot_cap, heads_rank, head_width)
            states, output = state_step(
                states,
                inner_heads,
                write_vec,
                read_vec,
                fresh_rate[:, :, :, step_idx],
                rate_shift,
                damping_log,
                skip_part,
            )
            outputs.append(
                output.reshape(rep_count, head_count, slot_cap, rank_width)
                .transpose(0, 2, 1, 3)
                .reshape(rep_count, slot_cap, head_count * rank_width)
            )
        per_layer.append(jnp.stack(outputs, axis=2).astype(jnp.bfloat16))
    return jnp.stack(per_layer, axis=2)[None, None]


def solution(mesh):
    return jax.shard_map(
        shards,
        mesh=mesh,
        in_specs=(
            P("rep", None, "head", None, None),
            P("rep", None, None, "head"),
            P("rep", None, None, None),
            P("rep", None),
            P("rep", "head", None, None, None, None, None),
            P("rep", None, None, None, None, None, None),
            P("rep", "head", None, None, None, None, None),
            P(),
            P(),
            P(),
            P(),
            P(),
            P(),
            P(),
        ),
        out_specs=P("rep", "head", None, None, None, None, None),
        check_vma=False,
    )
```

profile of v0, /device:TPU:1, one launch (start us, length us, event | category | flops | bytes accessed | tf_op | source)
XLA Modules:
  0.0 653.6 jit_solution(2088446739659863960)
XLA Ops:
  2.1 2.8 fusion.51
  7.1 2.0 slice_reduce_fusion.1
  9.1 1.3 gather_fusion.1
  10.4 1.3 gather_fusion.4
  12.1 0.9 maximum_select_fusion
  13.1 13.8 %all_to_all.40 = bf16[8,16,2,3,256]{4,1,3,2,0:T(8,128)(2,1)S(1)} all-to-all(bf16[8,16,2,3,256]{4,1,3,2,0:T(8,128)(2,1)S(1)} %get-tuple-element.85), channel_id=1, replica_groups=mesh['rep'=8,'head'=16] {'rep'}, dimensions={0} | all-to-all | bytes 786432 | tf_op jit(solution)/shard_map/all_to_all | solution.py:119
  26.9 4.2 all-to-all-start.6
  31.3 1.0 copy.509
  32.3 6.9 %all-to-all-done.6 = bf16[8,16,2,3,256]{4,1,3,2,0:T(8,128)(2,1)S(1)} async-done(((bf16[8,16,2,3,256]{4,1,3,2,0:T(8,128)(2,1)}), bf16[8,16,2,3,256]{4,1,3,2,0:T(8,128)(2,1)S(1)}, u32[]{:S(2)}, u32[]{:S(2)}) %all-to-all-start.6) | async-done | bytes 393248 | tf_op jit(solution)/shard_map/all_to_all | solution.py:119
  39.2 7.8 %all-to-all-start.3 = ((bf16[8,16,2,3,256]{4,0,3,2,1:T(8,128)(2,1)}), bf16[8,16,2,3,256]{4,0,3,2,1:T(8,128)(2,1)S(1)}, u32[]{:S(2)}, u32[]{:S(2)}) async-start(bf16[8,16,2,3,256]{4,0,3,2,1:T(8,128)(2,1)} %copy.509), calls=%async_computation.3 | async-start | bytes 786432 | tf_op jit(solution)/shard_map/all_to_all | solution.py:118
  47.1 7.3 %fusion.50 = (bf16[32,1,8,64,128]{4,3,2,1,0:T(8,128)(2,1)}, bf16[32,1,8,64,128]{4,3,2,1,0:T(8,128)(2,1)}) fusion(bf16[32,2,8,64,128]{4,3,2,1,0:T(8,128)(2,1)} %param.14), kind=kLoop, calls=%fused_computation.177 | loop fusion | bytes 16777216 | tf_op jit(solution)/shard_map/slice | solution.py:89
  54.4 12.0 %gather_fusion.3 = bf16[256,128,128]{2,1,0:T(8,128)(2,1)} fusion(bf16[32,4,128,128]{3,2,1,0:T(8,128)(2,1)} %bitcast.230, s32[256]{0:T(256)S(1)} %reshape.525), kind=kCustom, calls=%fused_computation.3 | custom fusion | bytes 16779264 | tf_op jit(solution)/shard_map/gather | solution.py:91
  66.4 11.9 %gather_fusion = bf16[256,128,128]{2,1,0:T(8,128)(2,1)} fusion(bf16[32,4,128,128]{3,2,1,0:T(8,128)(2,1)} %bitcast.229, s32[256]{0:T(256)S(1)} %reshape.525), kind=kCustom, calls=%fused_computation | custom fusion | bytes 16779264 | tf_op jit(solution)/shard_map/gather | solution.py:91
  78.3 1.0 copy.549
  79.2 6.8 %all-to-all-start.7 = ((bf16[8,16,2,3,256]{4,0,3,2,1:T(8,128)(2,1)}), bf16[8,16,2,3,256]{4,0,3,2,1:T(8,128)(2,1)S(1)}, u32[]{:S(2)}, u32[]{:S(2)}) async-start(bf16[8,16,2,3,256]{4,0,3,2,1:T(8,128)(2,1)} %copy.549), calls=%async_computation.7 | async-start | bytes 786432 | tf_op jit(solution)/shard_map/all_to_all | solution.py:118
  86.0 11.5 %broadcast_select_fusion.1 = (bf16[8,16,2,128,128]{4,3,2,1,0:T(8,128)(2,1)}, bf16[8,16,2,128,128]{4,3,2,1,0:T(8,128)(2,1)}) fusion(bf16[8,16,2,128,128]{4,3,2,1,0:T(8,128)(2,1)} %bitcast.232, pred[8,16,2]{2,1,0:T(8,128)(4,1)S(1)} %copy.495, bf16[8,16,2,128,128]{4,3,2,1,0:T(8,128)(2,1)} %bitcast.231), kind=kLoop, calls=%fused_computation.21 | loop fusion | flops 8388608 | bytes 33554688 | tf_op jit(solution)/shard_map/jit(_where)/select_n | solution.py:90
  97.5 102.3 %all_to_all.41 = bf16[8,16,2,128,128]{4,3,2,1,0:T(8,128)(2,1)} all-to-all(bf16[8,16,2,128,128]{4,3,2,1,0:T(8,128)(2,1)} %get-tuple-element.71), channel_id=1, replica_groups=mesh['rep'=8,'head'=16] {'rep'}, dimensions={0} | all-to-all | bytes 16777216 | tf_op jit(solution)/shard_map/all_to_all | solution.py:112
  199.8 5.9 all-to-all-start.4
  205.8 10.4 %copy.497 = bf16[8,16,2,128,128]{4,3,2,0,1:T(8,128)(2,1)} copy(bf16[8,16,2,128,128]{4,3,2,1,0:T(8,128)(2,1)} %all_to_all.41) | data formatting | bytes 16777216 | tf_op jit(solution)/shard_map/all_to_all | solution.py:112
  216.2 83.4 %all-to-all-done.4 = bf16[8,16,2,128,128]{4,3,2,1,0:T(8,128)(2,1)} async-done(((bf16[8,16,2,128,128]{4,3,2,1,0:T(8,128)(2,1)}), bf16[8,16,2,128,128]{4,3,2,1,0:T(8,128)(2,1)}, u32[]{:S(2)}, u32[]{:S(2)}) %all-to-all-start.4) | async-done | bytes 8388640 | tf_op jit(solution)/shard_map/all_to_all | solution.py:112
  299.6 7.5 %all-to-all-start.1 = ((bf16[8,16,2,128,128]{4,3,2,0,1:T(8,128)(2,1)}), bf16[8,16,2,128,128]{4,3,2,0,1:T(8,128)(2,1)}, u32[]{:S(2)}, u32[]{:S(2)}) async-start(bf16[8,16,2,128,128]{4,3,2,0,1:T(8,128)(2,1)} %copy.497), calls=%async_computation.1 | async-start | bytes 16777216 | tf_op jit(solution)/shard_map/all_to_all | solution.py:111
  316.1 10.3 %copy.539 = bf16[8,16,2,128,128]{4,3,2,0,1:T(8,128)(2,1)} copy(bf16[8,16,2,128,128]{4,3,2,1,0:T(8,128)(2,1)} %all-to-all-done.4) | data formatting | bytes 16777216 | tf_op jit(solution)/shard_map/all_to_all | solution.py:112
  326.4 103.1 %all-to-all-done.1 = bf16[8,16,2,128,128]{4,3,2,0,1:T(8,128)(2,1)} async-done(((bf16[8,16,2,128,128]{4,3,2,0,1:T(8,128)(2,1)}), bf16[8,16,2,128,128]{4,3,2,0,1:T(8,128)(2,1)}, u32[]{:S(2)}, u32[]{:S(2)}) %all-to-all-start.1) | async-done | bytes 8388640 | tf_op jit(solution)/shard_map/all_to_all | solution.py:111
  429.5 5.9 all-to-all-start.5
  440.6 13.8 %fusion.1 = (f32[8,16,2,2,64,128]{5,4,3,2,0,1:T(8,128)S(1)}, f32[8,16,2,2,64,128]{5,4,3,2,0,1:T(8,128)}) fusion(bf16[8,16,2,2,64,128]{5,4,3,2,0,1:T(8,128)(2,1)} %bitcast.87, f32[8,16,2,128]{3,2,0,1:T(2,128)S(1)} %bitcast.244, f32[8,16,2,2,64]{4,3,2,0,1:T(2,128)S(1)} %copy.516, f32[8,16,2,2]{3,2,0,1:T(2,128)S(1)} %copy.493, ...), kind=kLoop, calls=%fused_computation.9 | loop fusion | flops 29360128 | bytes 42471424 | tf_op jit(solution)/shard_map/add | solution.py:22
  454.5 41.5 %fusion.6 = f32[8,16,2,1,2,64]{5,3,4,2,1,0:T(1,128)S(1)} fusion(f32[8,16,2,2,64,128]{5,4,3,2,0,1:T(8,128)} %get-tuple-element.22, f32[8,16,2,128,1,1]{3,1,2,0,4,5:T(8,128)S(1)} %bitcast.248), kind=kOutput, calls=%fused_computation.14 | convolution fusion | flops 50331648 | bytes 17039360 | tf_op jit(solution)/shard_map/...upn,...n->...up/dot_general | solution.py:26
  496.1 39.5 %fusion.8 = f32[8,16,2,1,2,64]{5,3,4,2,1,0:T(1,128)S(1)} fusion(f32[8,16,2,2,64,128]{5,4,3,2,0,1:T(8,128)S(1)} %get-tuple-element.21, f32[8,16,2,128,1,1]{3,1,2,0,4,5:T(8,128)S(1)} %bitcast.249), kind=kOutput, calls=%fused_computation.16 | convolution fusion | flops 50331648 | bytes 17039360 | tf_op jit(solution)/shard_map/...upn,...n->...up/dot_general | solution.py:26
  536.6 19.5 %all-to-all-done.5 = bf16[8,16,2,128,128]{4,3,2,0,1:T(8,128)(2,1)} async-done(((bf16[8,16,2,128,128]{4,3,2,0,1:T(8,128)(2,1)}), bf16[8,16,2,128,128]{4,3,2,0,1:T(8,128)(2,1)}, u32[]{:S(2)}, u32[]{:S(2)}) %all-to-all-start.5) | async-done | bytes 8388640 | tf_op jit(solution)/shard_map/all_to_all | solution.py:111
  556.2 13.8 %fusion = (f32[8,16,2,2,64,128]{5,4,3,2,0,1:T(8,128)S(1)}, f32[8,16,2,2,64,128]{5,4,3,2,0,1:T(8,128)}) fusion(bf16[8,16,2,2,64,128]{5,4,3,2,0,1:T(8,128)(2,1)} %bitcast.97, f32[8,16,2,128]{3,2,0,1:T(2,128)S(1)} %bitcast.245, f32[8,16,2,2,64]{4,3,2,0,1:T(2,128)S(1)} %copy.556, f32[8,16,2,2]{3,2,0,1:T(2,128)S(1)} %copy.538, f32[8,16,2,128]{3,2,0,1:T(2,128)S(1)} %bitcast.247, ...), kind=kLoop, calls=%fused_computation.7 | loop fusion | flops 29360128 | bytes 42471424 | tf_op jit(solution)/shard_map/add | solution.py:22
  570.1 41.6 %fusion.2 = f32[8,16,2,1,2,64]{5,3,4,2,1,0:T(1,128)S(1)} fusion(f32[8,16,2,2,64,128]{5,4,3,2,0,1:T(8,128)} %get-tuple-element.24, f32[8,16,2,128,1,1]{3,1,2,0,4,5:T(8,128)S(1)} %bitcast.250), kind=kOutput, calls=%fused_computation.10 | convolution fusion | flops 50331648 | bytes 17039360 | tf_op jit(solution)/shard_map/...upn,...n->...up/dot_general | solution.py:26
  611.8 39.3 %fusion.4 = f32[8,16,2,1,2,64]{5,3,4,2,1,0:T(1,128)S(1)} fusion(f32[8,16,2,2,64,128]{5,4,3,2,0,1:T(8,128)S(1)} %get-tuple-element.23, f32[8,16,2,128,1,1]{3,1,2,0,4,5:T(8,128)S(1)} %bitcast.251), kind=kOutput, calls=%fused_computation.12 | convolution fusion | flops 50331648 | bytes 17039360 | tf_op jit(solution)/shard_map/...upn,...n->...up/dot_general | solution.py:26
  652.2 1.0 copy.573
  (201 shorter events, 20.7 us)
Async XLA Ops:
  0.0 309.0 %copy-start = (bf16[1,4,8,2,2,2,2048]{6,5,4,3,2,1,0:T(2,128)(2,1)S(1)}, bf16[1,4,8,2,2,2,2048]{6,5,4,3,2,1,0:T(2,128)(2,1)}, u32[]{:S(2)}) copy-start(bf16[1,4,8,2,2,2,2048]{6,5,4,3,2,1,0:T(2,128)(2,1)} %param.19) | copy-start | bytes 3145732
  26.9 12.3 %all-to-all-start.6 = ((bf16[8,16,2,3,256]{4,1,3,2,0:T(8,128)(2,1)}), bf16[8,16,2,3,256]{4,1,3,2,0:T(8,128)(2,1)S(1)}, u32[]{:S(2)}, u32[]{:S(2)}) async-start(bf16[8,16,2,3,256]{4,1,3,2,0:T(8,128)(2,1)} %get-tuple-element.86), calls=%async_computation.6 | async-start | bytes 786432 | tf_op jit(solution)/shard_map/all_to_all | solution.py:119
  39.2 40.0 %all-to-all-start.3 = ((bf16[8,16,2,3,256]{4,0,3,2,1:T(8,128)(2,1)}), bf16[8,16,2,3,256]{4,0,3,2,1:T(8,128)(2,1)S(1)}, u32[]{:S(2)}, u32[]{:S(2)}) async-start(bf16[8,16,2,3,256]{4,0,3,2,1:T(8,128)(2,1)} %copy.509), calls=%async_computation.3 | async-start | bytes 786432 | tf_op jit(solution)/shard_map/all_to_all | solution.py:118
  79.2 18.2 %all-to-all-start.7 = ((bf16[8,16,2,3,256]{4,0,3,2,1:T(8,128)(2,1)}), bf16[8,16,2,3,256]{4,0,3,2,1:T(8,128)(2,1)S(1)}, u32[]{:S(2)}, u32[]{:S(2)}) async-start(bf16[8,16,2,3,256]{4,0,3,2,1:T(8,128)(2,1)} %copy.549), calls=%async_computation.7 | async-start | bytes 786432 | tf_op jit(solution)/shard_map/all_to_all | solution.py:118
  199.8 99.7 %all-to-all-start.4 = ((bf16[8,16,2,128,128]{4,3,2,1,0:T(8,128)(2,1)}), bf16[8,16,2,128,128]{4,3,2,1,0:T(8,128)(2,1)}, u32[]{:S(2)}, u32[]{:S(2)}) async-start(bf16[8,16,2,128,128]{4,3,2,1,0:T(8,128)(2,1)} %get-tuple-element.72), calls=%async_computation.4 | async-start | bytes 16777216 | tf_op jit(solution)/shard_map/all_to_all | solution.py:112
  205.7 101.3 %copy-start.2 = (f32[2,4,8192]{2,1,0:T(4,128)S(1)}, f32[2,4,8192]{2,1,0:T(4,128)}, u32[]{:S(2)}) copy-start(f32[2,4,8192]{2,1,0:T(4,128)} %param.21) | copy-start | bytes 786436
  205.7 101.6 %copy-start.3 = (bf16[1,1,8,2,2,2,2048]{6,5,4,3,2,1,0:T(2,128)(2,1)S(1)}, bf16[1,1,8,2,2,2,2048]{6,5,4,3,2,1,0:T(2,128)(2,1)}, u32[]{:S(2)}) copy-start(bf16[1,1,8,2,2,2,2048]{6,5,4,3,2,1,0:T(2,128)(2,1)} %param.18) | copy-start | bytes 786436
  205.7 102.0 %copy-start.15 = (f32[2,128]{1,0:T(2,128)S(1)}, f32[2,128]{1,0:T(2,128)}, u32[]{:S(2)}) copy-start(f32[2,128]{1,0:T(2,128)} %param.25) | copy-start | bytes 3076
  205.7 102.5 %copy-start.16 = (f32[2,128]{1,0:T(2,128)S(1)}, f32[2,128]{1,0:T(2,128)}, u32[]{:S(2)}) copy-start(f32[2,128]{1,0:T(2,128)} %param.27) | copy-start | bytes 3076
  205.7 102.5 %copy-start.17 = (f32[2,128]{1,0:T(2,128)S(1)}, f32[2,128]{1,0:T(2,128)}, u32[]{:S(2)}) copy-start(f32[2,128]{1,0:T(2,128)} %param.26) | copy-start | bytes 3076
  205.7 102.8 %copy-start.11 = (bf16[1,1,8,2,2,2,32]{6,5,4,3,2,1,0:T(2,128)(2,1)S(1)}, bf16[1,1,8,2,2,2,32]{6,5,4,3,2,1,0:T(2,128)(2,1)}, u32[]{:S(2)}) copy-start(bf16[1,1,8,2,2,2,32]{6,5,4,3,2,1,0:T(2,128)(2,1)} %param.20) | copy-start | bytes 12292
  205.7 103.1 %copy-start.9 = (f32[2,8192]{1,0:T(2,128)S(1)}, f32[2,8192]{1,0:T(2,128)}, u32[]{:S(2)}) copy-start(f32[2,8192]{1,0:T(2,128)} %param.23) | copy-start | bytes 196612
  205.7 109.0 %copy-start.12 = (f32[2,2048]{1,0:T(2,128)S(1)}, f32[2,2048]{1,0:T(2,128)}, u32[]{:S(2)}) copy-start(f32[2,2048]{1,0:T(2,128)} %param.24) | copy-start | bytes 49156
  205.8 109.6 %copy-start.10 = (f32[2,4,2048]{2,1,0:T(4,128)S(1)}, f32[2,4,2048]{2,1,0:T(4,128)}, u32[]{:S(2)}) copy-start(f32[2,4,2048]{2,1,0:T(4,128)} %param.22) | copy-start | bytes 196612
  299.6 129.9 %all-to-all-start.1 = ((bf16[8,16,2,128,128]{4,3,2,0,1:T(8,128)(2,1)}), bf16[8,16,2,128,128]{4,3,2,0,1:T(8,128)(2,1)}, u32[]{:S(2)}, u32[]{:S(2)}) async-start(bf16[8,16,2,128,128]{4,3,2,0,1:T(8,128)(2,1)} %copy.497), calls=%async_computation.1 | async-start | bytes 16777216 | tf_op jit(solution)/shard_map/all_to_all | solution.py:111
  313.5 124.4 %copy-start.4 = (f32[16,2,64]{2,0,1:T(8,128)}, f32[16,2,64]{2,0,1:T(8,128)S(1)}, u32[]{:S(2)}) copy-start(f32[16,2,64]{2,0,1:T(8,128)S(1)} %copy.554) | copy-start | bytes 24580
  326.4 110.9 %copy-start.6 = (f32[4,16,1,128]{3,0,1,2:T(4,128)S(1)}, f32[4,16,1,128]{3,0,1,2:T(4,128)}, u32[]{:S(2)}) copy-start(f32[4,16,1,128]{3,0,1,2:T(4,128)} %copy.680) | copy-start | bytes 98308
  326.4 111.5 %copy-start.7 = (f32[8,16,2,2]{1,3,2,0:T(2,128)S(1)}, f32[8,16,2,2]{1,3,2,0:T(2,128)}, u32[]{:S(2)}) copy-start(f32[8,16,2,2]{1,3,2,0:T(2,128)} %copy.540) | copy-start | bytes 6148
  326.4 111.5 %copy-start.8 = (f32[8,16,2,2]{1,3,2,0:T(2,128)S(1)}, f32[8,16,2,2]{1,3,2,0:T(2,128)}, u32[]{:S(2)}) copy-start(f32[8,16,2,2]{1,3,2,0:T(2,128)} %copy.564) | copy-start | bytes 6148
  429.5 126.6 %all-to-all-start.5 = ((bf16[8,16,2,128,128]{4,3,2,0,1:T(8,128)(2,1)}), bf16[8,16,2,128,128]{4,3,2,0,1:T(8,128)(2,1)}, u32[]{:S(2)}, u32[]{:S(2)}) async-start(bf16[8,16,2,128,128]{4,3,2,0,1:T(8,128)(2,1)} %copy.539), calls=%async_computation.5 | async-start | bytes 16777216 | tf_op jit(solution)/shard_map/all_to_all | solution.py:111
  454.5 81.1 %copy-start.13 = (f32[16,1,2]{0,2,1:T(2,128)S(1)}, f32[16,1,2]{0,2,1:T(2,128)}, u32[]{:S(2)}) copy-start(f32[16,1,2]{0,2,1:T(2,128)} %copy.521) | copy-start | bytes 388
  570.1 83.1 %copy-start.1 = (bf16[1,4,8,2,2,2,2048]{6,5,4,3,2,1,0:T(2,128)(2,1)S(1)}, bf16[1,4,8,2,2,2,2048]{6,5,4,3,2,1,0:T(2,128)(2,1)}, u32[]{:S(2)}) copy-start(bf16[1,4,8,2,2,2,2048]{6,5,4,3,2,1,0:T(2,128)(2,1)} %param.19) | copy-start | bytes 3145732
  570.1 81.0 %copy-start.5 = (f32[16,2,64]{2,0,1:T(8,128)S(1)}, f32[16,2,64]{2,0,1:T(8,128)}, u32[]{:S(2)}) copy-start(f32[16,2,64]{2,0,1:T(8,128)} %copy-done.4) | copy-start | bytes 24580
  570.1 81.0 %copy-start.14 = (f32[16,1,2]{0,2,1:T(2,128)S(1)}, f32[16,1,2]{0,2,1:T(2,128)}, u32[]{:S(2)}) copy-start(f32[16,1,2]{0,2,1:T(2,128)} %copy.560) | copy-start | bytes 388
where the time goes:
time: 661 us; the launch traced here: 654 us
  waiting for transfers between devices  213 us (32%)
  matrix products  162 us (25%)
  blocking collectives  116 us (18%)
  local copies, waits for them, and re-layouts  77 us (12%)
  other arithmetic  46 us (7%)
  starting transfers between devices  38 us (6%)
    dot_general x4, matrix products, state_step(): jnp.einsum('...upn,...n->...up', states, read_vec, precision=lax.Precisio...  162 us
    all_to_all x2, waiting for transfers between devices, shards(): lax.all_to_all(lax.all_to_all(packed_states, 'rep', split_axis=0, concat_...  123 us
    all_to_all x1, blocking collectives, shards(): lax.all_to_all(packed_states, 'rep', split_axis=0, concat_axis=0, tiled=T...  102 us
    all_to_all x1, waiting for transfers between devices, shards(): lax.all_to_all(packed_states, 'rep', split_axis=0, concat_axis=0, tiled=T...  83.4 us
    add x2, other arithmetic, state_step(): damping[..., None, None] * states  27.6 us
    gather x2, local copies, waits for them, and re-layouts, shards(): local_states[source, rank_axis]  23.9 us
    all_to_all x2, local copies, waits for them, and re-layouts, shards(): lax.all_to_all(packed_states, 'rep', split_axis=0, concat_axis=0, tiled=T...  20.8 us
    all_to_all x2, starting transfers between devices, shards(): lax.all_to_all(lax.all_to_all(packed_tail, 'rep', split_axis=0, concat_ax...  14.6 us
  transfers between devices with their start and end apart: 6, of which 4 were waited for; matrix products, arithmetic and copies ran while one was open for 27% of the time, Pallas kernels for 0%

commit v1 on v0

v1 whole, which is shorter than its diff:
```python
import jax
import jax.numpy as jnp
from jax import lax
from jax.experimental import pallas as pl
from jax.experimental.pallas import tpu as pltpu
from jax.sharding import PartitionSpec as P

F32 = jnp.float32
BF16 = jnp.bfloat16
AXES = ("rep", "head")
N_REP, N_HEAD, TP, CAP, LAYERS, STEPS, KERNEL = 8, 16, 4, 2, 2, 2, 4
SUBS = N_HEAD // TP
REPLICAS = N_REP * SUBS
REQ = 32
HEADS = 128
HEADS_LOCAL = HEADS // N_HEAD
HEAD_DIM, STATE = 64, 128
WIDTH = HEADS_LOCAL * HEAD_DIM
RANK_WIDTH = WIDTH // TP
GROUP_SPAN = 1024
ROWS = CAP * LAYERS * STEPS
SLOT_ROWS = REPLICAS * ROWS
REQ_ROWS = REQ * LAYERS * STEPS
HIST_ROWS = REQ * (KERNEL - 1) * LAYERS
VMEM = pl.BlockSpec(memory_space=pltpu.VMEM)
HBM = pl.BlockSpec(memory_space=pltpu.HBM)


def iota(shape, dim):
    return lax.broadcasted_iota(jnp.int32, shape, dim)


def one_hot(cond):
    return jnp.where(cond, 1.0, 0.0).astype(BF16)


def dot(a, b):
    return jnp.dot(a, b, preferred_element_type=F32)


def split3(v):
    hi = v.astype(BF16)
    rest = v - hi.astype(F32)
    mid = rest.astype(BF16)
    return hi, mid, (rest - mid.astype(F32)).astype(BF16)


def pack_kernel(
    inner_hbm,
    group_hbm,
    rate_hbm,
    inner_tail_hbm,
    group_tail_hbm,
    chosen_hbm,
    conv_inner_hbm,
    conv_group_hbm,
    bias_inner_hbm,
    bias_group_hbm,
    rate_bias_hbm,
    decay_hbm,
    skip_hbm,
    states_hbm,
    out_ref,
    states_ref,
    part_ref,
    place_ref,
    taps_ref,
    params_ref,
    inner_buf,
    group_buf,
    rate_ref,
    rate_buf,
    hist_buf,
    inner_tail_ref,
    tail_b_ref,
    tail_c_ref,
    chosen_ref,
    conv_inner_ref,
    conv_b_ref,
    conv_c_ref,
    bias_inner_ref,
    bias_b_ref,
    bias_c_ref,
    rate_bias_ref,
    decay_ref,
    skip_ref,
    sems,
):
    pos = lax.axis_index("head")
    sub, rank = lax.div(pos, TP), lax.rem(pos, TP)
    quarter = group_hbm.at[0, sub, :, lax.div(rank, LAYERS), lax.rem(rank, LAYERS)]
    copies = [
        pltpu.make_async_copy(src, dst, sems.at[13 + n])
        for n, (src, dst) in enumerate(
            ((rate_hbm.at[0, 0], rate_ref), (quarter, group_buf), (inner_hbm.at[0, 0], inner_buf))
        )
    ]
    for copy in copies:
        copy.start()
    inner = pl.ds(pl.multiple_of(pos * WIDTH, WIDTH), WIDTH)
    b = pl.ds(pl.multiple_of(lax.div(pos, 2) * STATE, STATE), STATE)
    c = pl.ds(pl.multiple_of(GROUP_SPAN + lax.div(pos, 2) * STATE, STATE), STATE)
    moves = (
        (chosen_hbm, chosen_ref),
        (inner_tail_hbm, inner_tail_ref),
        (group_tail_hbm.at[:, :, :, b], tail_b_ref),
        (group_tail_hbm.at[:, :, :, c], tail_c_ref),
        (conv_inner_hbm.at[:, :, inner], conv_inner_ref),
        (conv_group_hbm.at[:, :, b], conv_b_ref),
        (conv_group_hbm.at[:, :, c], conv_c_ref),
        (bias_inner_hbm.at[:, inner], bias_inner_ref),
        (bias_group_hbm.at[:, b], bias_b_ref),
        (bias_group_hbm.at[:, c], bias_c_ref),
        (rate_bias_hbm, rate_bias_ref),
        (decay_hbm, decay_ref),
        (skip_hbm, skip_ref),
    )
    tails = [pltpu.make_async_copy(src, dst, sems.at[n]) for n, (src, dst) in enumerate(moves)]
    for copy in tails:
        copy.start()
    near = pltpu.make_async_copy(states_hbm, states_ref, sems.at[16])
    near.start()
    turn = (iota((ROWS, 128), 0) - 2 * rank) & 7
    copies[0].wait()
    for r in range(N_REP):
        rate_buf[r * ROWS : (r + 1) * ROWS] = jnp.concatenate(
            [rate_ref[r, c, l].astype(F32) for c in range(CAP) for l in range(LAYERS)], axis=0
        )
    rates = rate_buf[...].astype(BF16)
    rate_rows = jnp.zeros((N_HEAD, N_REP * 128), F32)
    for u in range(2):
        pick = one_hot(iota((N_HEAD, 2 * N_HEAD), 1) == 2 * iota((N_HEAD, 2 * N_HEAD), 0) + u)
        turned = lax.dot_general(
            pick, rates, (((1,), (1,)), ((), ())), preferred_element_type=F32
        ).astype(BF16)
        shape = (N_REP * ROWS, N_REP * 128)
        row, lane = iota(shape, 0), iota(shape, 1)
        place = one_hot(
            (row // ROWS == lane // 128) & (lane % 128 == 2 * (row % ROWS) + u)
        )
        rate_rows = rate_rows + dot(turned, place)
    copies[1].wait()
    copies[2].wait()
    for r in range(N_REP):
        inner = jnp.concatenate(
            [inner_buf[r, c, l].astype(F32) for c in range(CAP) for l in range(LAYERS)], axis=0
        ).astype(BF16)
        fresh = group_buf[r].astype(F32)
        for h in range(N_HEAD):
            out_ref[r, h, 0:ROWS, :] = inner[:, h * 128 : (h + 1) * 128]
            at = (h // 2) * 128
            b_new = fresh[:, at : at + 128]
            c_new = fresh[:, GROUP_SPAN + at : GROUP_SPAN + at + 128]
            tile = jnp.where(turn == 0, b_new[0:1], 0.0)
            tile = jnp.where(turn == 1, b_new[1:2], tile)
            tile = jnp.where(turn == 4, c_new[0:1], tile)
            tile = jnp.where(turn == 5, c_new[1:2], tile)
            tile = jnp.where(turn == 2, rate_rows[h : h + 1, r * 128 : (r + 1) * 128], tile)
            out_ref[r, h, ROWS : 2 * ROWS, :] = tile.astype(BF16)
    for copy in tails:
        copy.wait()
    for i in range(REQ):
        for j in range(KERNEL - 1):
            rows = slice((i * 3 + j) * 2, (i * 3 + j) * 2 + 2)
            hist_buf[rows, 0:WIDTH] = inner_tail_ref[i, j].astype(F32)
            hist_buf[rows, WIDTH : WIDTH + STATE] = tail_b_ref[i, j].astype(F32)
            hist_buf[rows, WIDTH + STATE :] = tail_c_ref[i, j].astype(F32)
    chosen = chosen_ref[...].astype(F32)
    ri, ci = iota((REQ, REQ), 0), iota((REQ, REQ), 1)
    column = jnp.sum(jnp.where(ri == ci, chosen, 0.0), axis=1, keepdims=True)
    before = jnp.where((column == chosen) & (ri < ci), 1.0, 0.0)
    slots = CAP * chosen + jnp.sum(before, axis=0, keepdims=True)
    slots = jnp.broadcast_to(slots, (8, REQ)).astype(BF16)
    wide = dot(slots, one_hot(iota((REQ, REQ_ROWS), 1) // 4 == iota((REQ, REQ_ROWS), 0)))[0:1]
    target = wide.astype(jnp.int32) * 4 + iota((1, REQ_ROWS), 1) % 4
    place_ref[...] = one_hot(iota((SLOT_ROWS, REQ_ROWS), 0) == target)
    wide = dot(slots, one_hot(iota((REQ, HIST_ROWS), 1) // 6 == iota((REQ, HIST_ROWS), 0)))[0:1]
    col = iota((1, HIST_ROWS), 1)
    col_key = wide.astype(jnp.int32) * 8 + (col % 2) * 4 + (col % 6) // 2
    row = iota((SLOT_ROWS, HIST_ROWS), 0)
    row_key = (row // 4) * 8 + ((row // 2) % 2) * 4 + row % 2
    hist = hist_buf[...].astype(BF16)
    second = (iota((ROWS, 1), 0) // 2) % 2 == 1
    later = iota((ROWS, 1), 0) % 2 == 1

    def by_layer(first, other):
        return jnp.where(second, other, first)

    def weight(tap):
        rows = [ref[:, tap : tap + 1, :] for ref in (conv_inner_ref, conv_b_ref, conv_c_ref)]
        return jnp.concatenate([by_layer(w[0], w[1]) for w in rows], axis=1)

    offset = jnp.concatenate(
        [by_layer(ref[0:1], ref[1:2]) for ref in (bias_inner_ref, bias_b_ref, bias_c_ref)], axis=1
    )
    total = jnp.broadcast_to(offset[None], (REPLICAS, ROWS, WIDTH + 2 * STATE))
    for tap in range(KERNEL - 1):
        window = dot(one_hot(row_key + tap == col_key), hist)
        total = total + weight(tap)[None] * window.reshape(REPLICAS, ROWS, WIDTH + 2 * STATE)
    part_ref[...] = total
    taps_ref[0] = jnp.where(later, weight(2), 0.0)
    taps_ref[1] = weight(3)
    spread = one_hot(
        iota((HEADS, WIDTH), 0) == pos * HEADS_LOCAL + iota((HEADS, WIDTH), 1) // HEAD_DIM
    )
    for n, ref in enumerate((rate_bias_ref, decay_ref, skip_ref)):
        both = by_layer(ref[0:1], ref[1:2])
        hi, mid, lo = split3(both)
        value = dot(hi, spread) + dot(mid, spread) + dot(lo, spread)
        params_ref[n] = jnp.exp(value) if n == 1 else value
    near.wait()


def step_kernel(
    got_ref,
    states_ref,
    part_ref,
    place_ref,
    taps_ref,
    params_ref,
    out_ref,
    read_buf,
    dots_buf,
    acc_buf,
    product_buf,
):
    pair = iota((1, ROWS, 128), 1) // 2
    later = iota((1, ROWS, 128), 1) % 2 == 1
    tap2_b = taps_ref[0, :, WIDTH : WIDTH + STATE][None]
    tap2_c = taps_ref[0, :, WIDTH + STATE :][None]
    tap3_b = taps_ref[1, :, WIDTH : WIDTH + STATE][None]
    tap3_c = taps_ref[1, :, WIDTH + STATE :][None]
    group = 4
    for q in range(0, REPLICAS, group):
        tiles = [got_ref[q : q + group, t, ROWS : 2 * ROWS, :].astype(F32) for t in range(TP)]
        b_new, c_new = tiles[0], tiles[2]
        for t in range(1, TP):
            b_new = jnp.where(pair == t, tiles[t], b_new)
            c_new = jnp.where(pair == t, tiles[(t + 2) % TP], c_new)
        c_new = pltpu.roll(c_new, 4, 1)
        b_act = part_ref[q : q + group, :, WIDTH : WIDTH + STATE]
        c_act = part_ref[q : q + group, :, WIDTH + STATE :]
        b_act = b_act + tap2_b * pltpu.roll(b_new, 1, 1) + tap3_b * b_new
        c_act = c_act + tap2_c * pltpu.roll(c_new, 1, 1) + tap3_c * c_new
        b_act = b_act * jax.nn.sigmoid(b_act)
        c_act = c_act * jax.nn.sigmoid(c_act)
        read_buf[q : q + group] = c_act
        same = jnp.sum(b_act * c_act, axis=2, keepdims=True)
        cross = jnp.sum(pltpu.roll(b_act, 1, 1) * c_act, axis=2, keepdims=True)
        dots_buf[0, q : q + group] = jnp.broadcast_to(same, (group, ROWS, 128))
        dots_buf[1, q : q + group] = jnp.broadcast_to(cross, (group, ROWS, 128))
    turned = read_buf[...].reshape(SLOT_ROWS, STATE).T
    hi = turned.astype(BF16)
    lo = (turned - hi.astype(F32)).astype(BF16)
    place = place_ref[...]
    columns = jnp.concatenate([dot(hi, place), dot(lo, place)], axis=1)
    owner = (iota((STATE, 2 * REQ_ROWS), 1) % REQ_ROWS) // 2
    per_chunk = 8
    for ch in range(REQ * LAYERS // per_chunk):
        span = range(ch * per_chunk, (ch + 1) * per_chunk)
        block = jnp.concatenate(
            [jnp.where(owner == m, columns, 0.0).astype(BF16) for m in span], axis=0
        )
        prod = dot(jnp.concatenate([states_ref[m] for m in span], axis=1), block)
        acc_buf[...] = prod if ch == 0 else acc_buf[...] + prod
    by_req = (acc_buf[:, 0:REQ_ROWS] + acc_buf[:, REQ_ROWS:]).T
    hi, mid, lo = split3(by_req)
    product_buf[...] = (dot(place, hi) + dot(place, mid) + dot(place, lo)).reshape(
        REPLICAS, ROWS, WIDTH
    )
    row, lane = iota((ROWS, 128), 0), iota((ROWS, 128), 1)
    mine = lane // 2 == row
    spread = one_hot(
        (iota((128, 128), 0) % 2 == iota((128, 128), 1) // HEAD_DIM) & (iota((128, 128), 0) < 16)
    )
    for t in range(TP):
        lanes = slice(t * RANK_WIDTH, (t + 1) * RANK_WIDTH)
        at = ROWS + (2 * t + 2) % ROWS
        tap2, tap3 = taps_ref[0, :, lanes][None], taps_ref[1, :, lanes][None]
        shift = params_ref[0, :, lanes][None]
        decay = params_ref[1, :, lanes][None]
        skip = params_ref[2, :, lanes][None]
        for q in range(0, REPLICAS, group):
            raw = got_ref[q : q + group, t, ROWS : 2 * ROWS, :].astype(F32)[
                :, at - ROWS : at - ROWS + 1, :
            ]
            raw = jnp.where(mine[None], raw, 0.0).astype(BF16).reshape(group * ROWS, 128)
            rate = dot(raw, spread).reshape(group, ROWS, 128) + shift
            dt = jnp.maximum(rate, 0.0) + jnp.log1p(jnp.exp(-jnp.abs(rate)))
            damp = jnp.exp(-dt * decay)
            fresh = got_ref[q : q + group, t, 0:ROWS, :].astype(F32)
            x = part_ref[q : q + group, :, lanes]
            x = x + tap2 * pltpu.roll(fresh, 1, 1) + tap3 * fresh
            x = x * jax.nn.sigmoid(x)
            taken = dt * x
            before = jnp.where(later, pltpu.roll(damp, 1, 1), 1.0)
            carried = jnp.where(later, pltpu.roll(taken, 1, 1) * dots_buf[1, q : q + group], 0.0)
            y = damp * (before * product_buf[q : q + group, :, lanes] + carried)
            y = y + taken * dots_buf[0, q : q + group] + skip * x
            out_ref[q : q + group, t] = y.astype(BF16)


def unpack_kernel(got_ref, out_ref):
    for r in range(N_REP):
        rows = jnp.concatenate([got_ref[r, h].astype(F32) for h in range(N_HEAD)], axis=1)
        for c in range(CAP):
            for l in range(LAYERS):
                at = (c * LAYERS + l) * STEPS
                out_ref[0, 0, r, c, l] = rows[at : at + STEPS].astype(BF16)


def shards(
    prefill_states,
    inner_tail,
    group_tail,
    assignment,
    decode_inner,
    decode_groups,
    decode_rate,
    conv_inner,
    conv_group,
    bias_inner,
    bias_group,
    rate_bias,
    decay_log,
    skip_gain,
):
    tail = (REQ, KERNEL - 1, LAYERS)
    packed, states, part, place, taps, params = pl.pallas_call(
        pack_kernel,
        out_shape=(
            jax.ShapeDtypeStruct((N_REP, N_HEAD, 2 * ROWS, 128), BF16),
            jax.ShapeDtypeStruct((REQ * LAYERS, WIDTH, STATE), BF16),
            jax.ShapeDtypeStruct((REPLICAS, ROWS, WIDTH + 2 * STATE), F32),
            jax.ShapeDtypeStruct((SLOT_ROWS, REQ_ROWS), BF16),
            jax.ShapeDtypeStruct((2, ROWS, WIDTH + 2 * STATE), F32),
            jax.ShapeDtypeStruct((3, ROWS, WIDTH), F32),
        ),
        in_specs=[HBM] * 14,
        out_specs=(VMEM,) * 6,
        scratch_shapes=[
            pltpu.VMEM(decode_inner.shape[2:], BF16),
            pltpu.VMEM((N_REP, STEPS, 2 * GROUP_SPAN), BF16),
            pltpu.VMEM(decode_rate.shape[2:], BF16),
            pltpu.VMEM((N_REP * ROWS, 2 * N_HEAD), F32),
            pltpu.VMEM((HIST_ROWS, WIDTH + 2 * STATE), F32),
            pltpu.VMEM(tail + (WIDTH,), BF16),
            pltpu.VMEM(tail + (STATE,), BF16),
            pltpu.VMEM(tail + (STATE,), BF16),
            pltpu.VMEM((1, REQ), jnp.int32),
            pltpu.VMEM((LAYERS, KERNEL, WIDTH), F32),
            pltpu.VMEM((LAYERS, KERNEL, STATE), F32),
            pltpu.VMEM((LAYERS, KERNEL, STATE), F32),
            pltpu.VMEM((LAYERS, WIDTH), F32),
            pltpu.VMEM((LAYERS, STATE), F32),
            pltpu.VMEM((LAYERS, STATE), F32),
            pltpu.VMEM((LAYERS, HEADS), F32),
            pltpu.VMEM((LAYERS, HEADS), F32),
            pltpu.VMEM((LAYERS, HEADS), F32),
            pltpu.SemaphoreType.DMA((17,)),
        ],
        compiler_params=pltpu.CompilerParams(vmem_limit_bytes=16 << 20),
        name="pack",
    )(
        *[
            pltpu.with_memory_space_constraint(v, pltpu.HBM)
            for v in (
                decode_inner,
                decode_groups,
                decode_rate,
                inner_tail.transpose(0, 2, 1, 3),
                group_tail.transpose(0, 2, 1, 3),
                assignment.reshape(1, REQ),
                conv_inner,
                conv_group,
                bias_inner,
                bias_group,
                rate_bias,
                decay_log,
                skip_gain,
                prefill_states.reshape(REQ * LAYERS, WIDTH, STATE),
            )
        ]
    )
    got = lax.all_to_all(
        packed.reshape(N_REP * N_HEAD, 2 * ROWS, 128), AXES, 0, 0, tiled=True
    ).reshape(REPLICAS, TP, 2 * ROWS, 128)
    decoded = pl.pallas_call(
        step_kernel,
        out_shape=jax.ShapeDtypeStruct((REPLICAS, TP, ROWS, 128), BF16),
        in_specs=[VMEM] * 6,
        out_specs=VMEM,
        scratch_shapes=[
            pltpu.VMEM((REPLICAS, ROWS, STATE), F32),
            pltpu.VMEM((2, REPLICAS, ROWS, 128), F32),
            pltpu.VMEM((WIDTH, 2 * REQ_ROWS), F32),
            pltpu.VMEM((REPLICAS, ROWS, WIDTH), F32),
        ],
        compiler_params=pltpu.CompilerParams(vmem_limit_bytes=16 << 20),
        name="step",
    )(got, states, part, place, taps, params)
    back = lax.all_to_all(
        decoded.reshape(REPLICAS * TP, ROWS, 128), AXES, 0, 0, tiled=True
    ).reshape(N_REP, N_HEAD, ROWS, 128)
    return pl.pallas_call(
        unpack_kernel,
        out_shape=jax.ShapeDtypeStruct((1, 1, N_REP, CAP, LAYERS, STEPS, N_HEAD * 128), BF16),
        in_specs=[VMEM],
        out_specs=VMEM,
        compiler_params=pltpu.CompilerParams(vmem_limit_bytes=16 << 20),
        name="unpack",
    )(back)


def solution(mesh):
    return jax.shard_map(
        shards,
        mesh=mesh,
        in_specs=(
            P("rep", None, "head", None, None),
            P("rep", None, None, "head"),
            P("rep", None, None, None),
            P("rep", None),
            P("rep", "head", None, None, None, None, None),
            P("rep", None, None, None, None, None, None),
            P("rep", "head", None, None, None, None, None),
            P(),
            P(),
            P(),
            P(),
            P(),
            P(),
            P(),
        ),
        out_specs=P("rep", "head", None, None, None, None, None),
        check_vma=False,
    )
```

time: 661 us -> 49.6 us (0.08); the launches traced: 654 us -> 49.4 us
  waiting for transfers between devices: 213 us -> 0 us
  matrix products: 162 us -> 0 us
  local copies, waits for them, and re-layouts: 77 us -> 0 us
  blocking collectives: 116 us -> 40.7 us
  other arithmetic: 46 us -> 0 us
  starting transfers between devices: 38 us -> 0 us
  Pallas kernels: 0 us -> 8.76 us
    all_to_all x6 -> x0, waiting for transfers between devices: 213 us -> none  [the longest x2 123 us: shards(): lax.all_to_all(lax.all_to_all(packed_states, 'rep', split_axis=0, concat_...]
    dot_general x4 -> x0, matrix products: 162 us -> none  [state_step(): jnp.einsum('...upn,...n->...up', states, read_vec, precision=lax.Precisio...]
    all_to_all x2, blocking collectives: 116 us -> 40.7 us  [the longest x1 25.4 us: shards(): lax.all_to_all(packed.reshape(N_REP * N_HEAD, 2 * ROWS, 128), AXES, 0, 0,...]
    all_to_all x6 -> x0, starting transfers between devices: 38 us -> none  [the longest x2 14.6 us: shards(): lax.all_to_all(lax.all_to_all(packed_tail, 'rep', split_axis=0, concat_ax...]
    gather x6 -> x0, local copies, waits for them, and re-layouts: 27.7 us -> none  [the longest x2 23.9 us: shards(): local_states[source, rank_axis]]
    add x2 -> x0, other arithmetic: 27.6 us -> none  [state_step(): damping[..., None, None] * states]
    all_to_all x4 -> x0, local copies, waits for them, and re-layouts: 22.7 us -> none  [the longest x2 20.8 us: shards(): lax.all_to_all(packed_states, 'rep', split_axis=0, concat_axis=0, tiled=T...]
    slice x22 -> x0, local copies, waits for them, and re-layouts: 13.5 us -> none  [the longest x1 7.33 us: shards(): prefill_states[:, layer_idx].reshape(req_local, TP, rank_width, state_width)]
  transfers between devices with their start and end apart: 6 -> 0, of which waited for: 4 -> 0; matrix products, arithmetic and copies ran while one was open for 27% -> 0% of each run, Pallas kernels for 0% -> 0%
where the time goes in v1:
time: 49.6 us; the launch traced here: 49.4 us
  blocking collectives  40.7 us (82%)
  Pallas kernels  8.76 us (18%)
    all_to_all x1, blocking collectives, shards(): lax.all_to_all(packed.reshape(N_REP * N_HEAD, 2 * ROWS, 128), AXES, 0, 0,...  25.4 us
    all_to_all x1, blocking collectives, shards(): lax.all_to_all(decoded.reshape(REPLICAS * TP, ROWS, 128), AXES, 0, 0, til...  15.2 us
    pallas_call x1, Pallas kernels, shards(): pl.pallas_call(step_kernel, out_shape=jax.ShapeDtypeStruct((REPLICAS, TP,...  4.12 us
    pallas_call x1, Pallas kernels, shards(): pl.pallas_call(pack_kernel, out_shape=(jax.ShapeDtypeStruct((N_REP, N_HEA...  3.9 us

profile of v1, /device:TPU:1, one launch (start us, length us, event | category | flops | bytes accessed | tf_op | source)
XLA Modules:
  0.0 49.4 jit_solution(15720109028366777778)
XLA Ops:
  0.0 3.9 %pack.1 = (bf16[8,16,16,128]{3,2,1,0:T(8,128)(2,1)S(1)}, bf16[64,512,128]{2,1,0:T(8,128)(2,1)S(1)}, f32[32,8,768]{2,1,0:T(8,128)S(1)}, bf16[256,128]{1,0:T(8,128...) custom-call(bf16[1,1,8,2,2,2,2048]{6,5,4,3,2,1,0:T(2,128)(2,1)} %inner_hbm.1, ...), custom_call_target="tpu_custom_call" | custom-call | tf_op jit(solution)/shard_map/pack/pallas_call | solution.py:329
  3.9 25.4 %all_to_all.10 = bf16[128,16,128]{2,1,0:T(8,128)(2,1)S(1)} all-to-all(bf16[128,16,128]{2,1,0:T(8,128)(2,1)S(1)} %bitcast.11), channel_id=1, replica_groups=mesh['rep'=8,'head'=16] {'rep','head'}, dimensions={0} | all-to-all | bytes 1048576 | tf_op jit(solution)/shard_map/all_to_all | solution.py:385
  29.3 4.1 %step.1 = bf16[32,4,8,128]{3,2,1,0:T(8,128)(2,1)S(1)} custom-call(bf16[32,4,16,128]{3,2,1,0:T(8,128)(2,1)S(1)} %bitcast.8, bf16[64,512,128]{2,1,0:T(8,128)(2,1)S(1)} %get-tuple-element.12.states_ref, f32[32,8,768]{2,1,0:T(8,128)S(1)} %get-tuple-element.13.part_ref, bf16[256,128]{1,0:T(8,128)(2,1)S(1)} %get-tuple-element.14.place_ref, ...), custom_call_target="tpu_custom_call" | custom-call | tf_op jit(solution)/shard_map/step/pallas_call | solution.py:388
  33.5 15.2 %all_to_all.11 = bf16[128,8,128]{2,1,0:T(8,128)(2,1)S(1)} all-to-all(bf16[128,8,128]{2,1,0:T(8,128)(2,1)S(1)} %bitcast.9), channel_id=1, replica_groups=mesh['rep'=8,'head'=16] {'rep','head'}, dimensions={0} | all-to-all | bytes 524288 | tf_op jit(solution)/shard_map/all_to_all | solution.py:402
  48.7 0.7 %unpack.1 = bf16[1,1,8,2,2,2,2048]{6,5,4,3,2,1,0:T(2,128)(2,1)} custom-call(bf16[8,16,8,128]{3,2,1,0:T(8,128)(2,1)S(1)} %bitcast.10), custom_call_target="tpu_custom_call" | custom-call | tf_op jit(solution)/shard_map/unpack/pallas_call | solution.py:405

commit v2 on v1

--- a/solution.py
+++ b/solution.py
@@ -20,9 +20,9 @@
 GROUP_SPAN = 1024
 ROWS = CAP * LAYERS * STEPS
 SLOT_ROWS = REPLICAS * ROWS
-REQ_ROWS = REQ * LAYERS * STEPS
 HIST_ROWS = REQ * (KERNEL - 1) * LAYERS
 VMEM = pl.BlockSpec(memory_space=pltpu.VMEM)
+SMEM = pl.BlockSpec(memory_space=pltpu.SMEM)
 HBM = pl.BlockSpec(memory_space=pltpu.HBM)
 
 
@@ -62,8 +62,8 @@
     states_hbm,
     out_ref,
     states_ref,
+    slots_ref,
     part_ref,
-    place_ref,
     taps_ref,
     params_ref,
     inner_buf,
@@ -84,6 +84,8 @@
     rate_bias_ref,
     decay_ref,
     skip_ref,
+    listing,
+    counts,
     sems,
 ):
     pos = lax.axis_index("head")
@@ -120,6 +122,10 @@
         copy.start()
     near = pltpu.make_async_copy(states_hbm, states_ref, sems.at[16])
     near.start()
+    listed = pltpu.make_async_copy(chosen_hbm, listing, sems.at[17])
+    listed.start()
+    for q in range(REPLICAS):
+        counts[q] = 0
     turn = (iota((ROWS, 128), 0) - 2 * rank) & 7
     copies[0].wait()
     for r in range(N_REP):
@@ -165,15 +171,18 @@
             hist_buf[rows, 0:WIDTH] = inner_tail_ref[i, j].astype(F32)
             hist_buf[rows, WIDTH : WIDTH + STATE] = tail_b_ref[i, j].astype(F32)
             hist_buf[rows, WIDTH + STATE :] = tail_c_ref[i, j].astype(F32)
+    listed.wait()
+    for i in range(REQ):
+        q = listing[0, i]
+        rank = counts[q]
+        slots_ref[i] = CAP * q + rank
+        counts[q] = rank + 1
     chosen = chosen_ref[...].astype(F32)
     ri, ci = iota((REQ, REQ), 0), iota((REQ, REQ), 1)
     column = jnp.sum(jnp.where(ri == ci, chosen, 0.0), axis=1, keepdims=True)
     before = jnp.where((column == chosen) & (ri < ci), 1.0, 0.0)
     slots = CAP * chosen + jnp.sum(before, axis=0, keepdims=True)
     slots = jnp.broadcast_to(slots, (8, REQ)).astype(BF16)
-    wide = dot(slots, one_hot(iota((REQ, REQ_ROWS), 1) // 4 == iota((REQ, REQ_ROWS), 0)))[0:1]
-    target = wide.astype(jnp.int32) * 4 + iota((1, REQ_ROWS), 1) % 4
-    place_ref[...] = one_hot(iota((SLOT_ROWS, REQ_ROWS), 0) == target)
     wide = dot(slots, one_hot(iota((REQ, HIST_ROWS), 1) // 6 == iota((REQ, HIST_ROWS), 0)))[0:1]
     col = iota((1, HIST_ROWS), 1)
     col_key = wide.astype(jnp.int32) * 8 + (col % 2) * 4 + (col % 6) // 2
@@ -214,18 +223,18 @@
 def step_kernel(
     got_ref,
     states_ref,
+    slots_ref,
     part_ref,
-    place_ref,
     taps_ref,
     params_ref,
     out_ref,
     read_buf,
     dots_buf,
-    acc_buf,
     product_buf,
 ):
     pair = iota((1, ROWS, 128), 1) // 2
     later = iota((1, ROWS, 128), 1) % 2 == 1
+    layer = (iota((1, 2 * ROWS, 128), 1) // STEPS) % LAYERS
     tap2_b = taps_ref[0, :, WIDTH : WIDTH + STATE][None]
     tap2_c = taps_ref[0, :, WIDTH + STATE :][None]
     tap3_b = taps_ref[1, :, WIDTH : WIDTH + STATE][None]
@@ -244,30 +253,24 @@
         c_act = c_act + tap2_c * pltpu.roll(c_new, 1, 1) + tap3_c * c_new
         b_act = b_act * jax.nn.sigmoid(b_act)
         c_act = c_act * jax.nn.sigmoid(c_act)
-        read_buf[q : q + group] = c_act
+        hi = c_act.astype(BF16).astype(F32)
+        both = jnp.concatenate([hi, c_act - hi], axis=1)
+        halves = [jnp.where(layer == l, both, 0.0) for l in range(LAYERS)]
+        read_buf[q : q + group] = jnp.concatenate(halves, axis=2).astype(BF16)
         same = jnp.sum(b_act * c_act, axis=2, keepdims=True)
         cross = jnp.sum(pltpu.roll(b_act, 1, 1) * c_act, axis=2, keepdims=True)
         dots_buf[0, q : q + group] = jnp.broadcast_to(same, (group, ROWS, 128))
         dots_buf[1, q : q + group] = jnp.broadcast_to(cross, (group, ROWS, 128))
-    turned = read_buf[...].reshape(SLOT_ROWS, STATE).T
-    hi = turned.astype(BF16)
-    lo = (turned - hi.astype(F32)).astype(BF16)
-    place = place_ref[...]
-    columns = jnp.concatenate([dot(hi, place), dot(lo, place)], axis=1)
-    owner = (iota((STATE, 2 * REQ_ROWS), 1) % REQ_ROWS) // 2
-    per_chunk = 8
-    for ch in range(REQ * LAYERS // per_chunk):
-        span = range(ch * per_chunk, (ch + 1) * per_chunk)
-        block = jnp.concatenate(
-            [jnp.where(owner == m, columns, 0.0).astype(BF16) for m in span], axis=0
+    product_buf[...] = jnp.zeros_like(product_buf)
+    rank_of_row = iota((ROWS, WIDTH), 0) // (LAYERS * STEPS)
+    for i in range(REQ):
+        q, rank = lax.shift_right_logical(slots_ref[i], 1), slots_ref[i] & 1
+        state = jnp.concatenate([states_ref[i * LAYERS + l] for l in range(LAYERS)], axis=1)
+        prod = lax.dot_general(
+            read_buf[q], state, (((1,), (1,)), ((), ())), preferred_element_type=F32
         )
-        prod = dot(jnp.concatenate([states_ref[m] for m in span], axis=1), block)
-        acc_buf[...] = prod if ch == 0 else acc_buf[...] + prod
-    by_req = (acc_buf[:, 0:REQ_ROWS] + acc_buf[:, REQ_ROWS:]).T
-    hi, mid, lo = split3(by_req)
-    product_buf[...] = (dot(place, hi) + dot(place, mid) + dot(place, lo)).reshape(
-        REPLICAS, ROWS, WIDTH
-    )
+        prod = prod[0:ROWS] + prod[ROWS:]
+        product_buf[q] = product_buf[q] + jnp.where(rank_of_row == rank, prod, 0.0)
     row, lane = iota((ROWS, 128), 0), iota((ROWS, 128), 1)
     mine = lane // 2 == row
     spread = one_hot(
@@ -325,19 +328,23 @@
     decay_log,
     skip_gain,
 ):
+    states = pltpu.with_memory_space_constraint(
+        prefill_states.reshape(REQ * LAYERS, WIDTH, STATE), pltpu.HBM
+    )
+    chosen = pltpu.with_memory_space_constraint(assignment.reshape(1, REQ), pltpu.HBM)
     tail = (REQ, KERNEL - 1, LAYERS)
-    packed, states, part, place, taps, params = pl.pallas_call(
+    packed, near, slots, part, taps, params = pl.pallas_call(
         pack_kernel,
         out_shape=(
             jax.ShapeDtypeStruct((N_REP, N_HEAD, 2 * ROWS, 128), BF16),
             jax.ShapeDtypeStruct((REQ * LAYERS, WIDTH, STATE), BF16),
+            pltpu.SMEM((REQ,), jnp.int32),
             jax.ShapeDtypeStruct((REPLICAS, ROWS, WIDTH + 2 * STATE), F32),
-            jax.ShapeDtypeStruct((SLOT_ROWS, REQ_ROWS), BF16),
             jax.ShapeDtypeStruct((2, ROWS, WIDTH + 2 * STATE), F32),
             jax.ShapeDtypeStruct((3, ROWS, WIDTH), F32),
         ),
         in_specs=[HBM] * 14,
-        out_specs=(VMEM,) * 6,
+        out_specs=(VMEM, VMEM, SMEM, VMEM, VMEM, VMEM),
         scratch_shapes=[
             pltpu.VMEM(decode_inner.shape[2:], BF16),
             pltpu.VMEM((N_REP, STEPS, 2 * GROUP_SPAN), BF16),
@@ -357,7 +364,9 @@
             pltpu.VMEM((LAYERS, HEADS), F32),
             pltpu.VMEM((LAYERS, HEADS), F32),
             pltpu.VMEM((LAYERS, HEADS), F32),
-            pltpu.SemaphoreType.DMA((17,)),
+            pltpu.SMEM((1, REQ), jnp.int32),
+            pltpu.SMEM((REPLICAS,), jnp.int32),
+            pltpu.SemaphoreType.DMA((18,)),
         ],
         compiler_params=pltpu.CompilerParams(vmem_limit_bytes=16 << 20),
         name="pack",
@@ -370,7 +379,7 @@
                 decode_rate,
                 inner_tail.transpose(0, 2, 1, 3),
                 group_tail.transpose(0, 2, 1, 3),
-                assignment.reshape(1, REQ),
+                chosen,
                 conv_inner,
                 conv_group,
                 bias_inner,
@@ -378,7 +387,7 @@
                 rate_bias,
                 decay_log,
                 skip_gain,
-                prefill_states.reshape(REQ * LAYERS, WIDTH, STATE),
+                states,
             )
         ]
     )
@@ -388,17 +397,16 @@
     decoded = pl.pallas_call(
         step_kernel,
         out_shape=jax.ShapeDtypeStruct((REPLICAS, TP, ROWS, 128), BF16),
-        in_specs=[VMEM] * 6,
+        in_specs=[VMEM, VMEM, SMEM, VMEM, VMEM, VMEM],
         out_specs=VMEM,
         scratch_shapes=[
-            pltpu.VMEM((REPLICAS, ROWS, STATE), F32),
+            pltpu.VMEM((REPLICAS, 2 * ROWS, LAYERS * STATE), BF16),
             pltpu.VMEM((2, REPLICAS, ROWS, 128), F32),
-            pltpu.VMEM((WIDTH, 2 * REQ_ROWS), F32),
             pltpu.VMEM((REPLICAS, ROWS, WIDTH), F32),
         ],
-        compiler_params=pltpu.CompilerParams(vmem_limit_bytes=16 << 20),
+        compiler_params=pltpu.CompilerParams(vmem_limit_bytes=20 << 20),
         name="step",
-    )(got, states, part, place, taps, params)
+    )(got, near, slots, part, taps, params)
     back = lax.all_to_all(
         decoded.reshape(REPLICAS * TP, ROWS, 128), AXES, 0, 0, tiled=True
     ).reshape(N_REP, N_HEAD, ROWS, 128)

time: 49.6 us -> 48.7 us (0.982)
  Pallas kernels: 8.76 us -> 7.77 us
    pallas_call x1, Pallas kernels: 4.12 us -> 3.13 us  [shards(): pl.pallas_call(step_kernel, out_shape=jax.ShapeDtypeStruct((REPLICAS, TP,...]
where the time goes in v2:
time: 48.7 us; the launch traced here: 48.5 us
  blocking collectives  40.7 us (84%)
  Pallas kernels  7.77 us (16%)
    all_to_all x1, blocking collectives, shards(): lax.all_to_all(packed.reshape(N_REP * N_HEAD, 2 * ROWS, 128), AXES, 0, 0,...  25.4 us
    all_to_all x1, blocking collectives, shards(): lax.all_to_all(decoded.reshape(REPLICAS * TP, ROWS, 128), AXES, 0, 0, til...  15.2 us
    pallas_call x1, Pallas kernels, shards(): pl.pallas_call(pack_kernel, out_shape=(jax.ShapeDtypeStruct((N_REP, N_HEA...  3.91 us
    pallas_call x1, Pallas kernels, shards(): pl.pallas_call(step_kernel, out_shape=jax.ShapeDtypeStruct((REPLICAS, TP,...  3.13 us

profile of v2, /device:TPU:1, one launch (start us, length us, event | category | flops | bytes accessed | tf_op | source)
XLA Modules:
  0.0 48.5 jit_solution(15584876396832495018)
XLA Ops:
  0.0 3.9 %pack.1 = (bf16[8,16,16,128]{3,2,1,0:T(8,128)(2,1)S(1)}, bf16[64,512,128]{2,1,0:T(8,128)(2,1)S(1)}, s32[32]{0:T(128)S(4)}, f32[32,8,768]{2,1,0:T(8,128)S(1)}, f3...) custom-call(bf16[1,1,8,2,2,2,2048]{6,5,4,3,2,1,0:T(2,128)(2,1)} %inner_hbm.1, ...), custom_call_target="tpu_custom_call" | custom-call | tf_op jit(solution)/shard_map/pack/pallas_call | solution.py:336
  3.9 25.4 %all_to_all.10 = bf16[128,16,128]{2,1,0:T(8,128)(2,1)S(1)} all-to-all(bf16[128,16,128]{2,1,0:T(8,128)(2,1)S(1)} %bitcast.11), channel_id=1, replica_groups=mesh['rep'=8,'head'=16] {'rep','head'}, dimensions={0} | all-to-all | bytes 1048576 | tf_op jit(solution)/shard_map/all_to_all | solution.py:394
  29.3 3.1 %step.1 = bf16[32,4,8,128]{3,2,1,0:T(8,128)(2,1)S(1)} custom-call(bf16[32,4,16,128]{3,2,1,0:T(8,128)(2,1)S(1)} %bitcast.8, bf16[64,512,128]{2,1,0:T(8,128)(2,1)S(1)} %get-tuple-element.12.states_ref, s32[32]{0:T(128)S(4)} %get-tuple-element.13.slots_ref, f32[32,8,768]{2,1,0:T(8,128)S(1)} %get-tuple-element.14.part_ref, ...), custom_call_target="tpu_custom_call" | custom-call | tf_op jit(solution)/shard_map/step/pallas_call | solution.py:397
  32.5 15.2 %all_to_all.11 = bf16[128,8,128]{2,1,0:T(8,128)(2,1)S(1)} all-to-all(bf16[128,8,128]{2,1,0:T(8,128)(2,1)S(1)} %bitcast.9), channel_id=1, replica_groups=mesh['rep'=8,'head'=16] {'rep','head'}, dimensions={0} | all-to-all | bytes 524288 | tf_op jit(solution)/shard_map/all_to_all | solution.py:410
  47.7 0.7 %unpack.1 = bf16[1,1,8,2,2,2,2048]{6,5,4,3,2,1,0:T(2,128)(2,1)} custom-call(bf16[8,16,8,128]{3,2,1,0:T(8,128)(2,1)S(1)} %bitcast.10), custom_call_target="tpu_custom_call" | custom-call | tf_op jit(solution)/shard_map/unpack/pallas_call | solution.py:413

commit v3 on v2

--- a/solution.py
+++ b/solution.py
@@ -20,6 +20,9 @@
 GROUP_SPAN = 1024
 ROWS = CAP * LAYERS * STEPS
 SLOT_ROWS = REPLICAS * ROWS
+FAR = 14
+NEAR = REQ - FAR
+PIECE = 7
 HIST_ROWS = REQ * (KERNEL - 1) * LAYERS
 VMEM = pl.BlockSpec(memory_space=pltpu.VMEM)
 SMEM = pl.BlockSpec(memory_space=pltpu.SMEM)
@@ -120,12 +123,15 @@
     tails = [pltpu.make_async_copy(src, dst, sems.at[n]) for n, (src, dst) in enumerate(moves)]
     for copy in tails:
         copy.start()
-    near = pltpu.make_async_copy(states_hbm, states_ref, sems.at[16])
-    near.start()
     listed = pltpu.make_async_copy(chosen_hbm, listing, sems.at[17])
     listed.start()
-    for q in range(REPLICAS):
+    near = pltpu.make_async_copy(states_hbm.at[pl.ds(0, NEAR * LAYERS)], states_ref, sems.at[16])
+    near.start()
+
+    @pl.loop(0, REPLICAS)
+    def _(q):
         counts[q] = 0
+
     turn = (iota((ROWS, 128), 0) - 2 * rank) & 7
     copies[0].wait()
     for r in range(N_REP):
@@ -222,7 +228,8 @@
 
 def step_kernel(
     got_ref,
-    states_ref,
+    near_ref,
+    states_hbm,
     slots_ref,
     part_ref,
     taps_ref,
@@ -231,7 +238,22 @@
     read_buf,
     dots_buf,
     product_buf,
+    base_buf,
+    gain_buf,
+    far_buf,
+    sems,
 ):
+    def fetch(n):
+        return pltpu.make_async_copy(
+            states_hbm.at[pl.ds((NEAR + n * PIECE) * LAYERS, PIECE * LAYERS)],
+            far_buf.at[pl.ds(n * PIECE * LAYERS, PIECE * LAYERS)],
+            sems.at[n],
+        )
+
+    @pl.loop(0, FAR // PIECE)
+    def _(n):
+        fetch(n).start()
+
     pair = iota((1, ROWS, 128), 1) // 2
     later = iota((1, ROWS, 128), 1) % 2 == 1
     layer = (iota((1, 2 * ROWS, 128), 1) // STEPS) % LAYERS
@@ -262,44 +284,53 @@
         dots_buf[0, q : q + group] = jnp.broadcast_to(same, (group, ROWS, 128))
         dots_buf[1, q : q + group] = jnp.broadcast_to(cross, (group, ROWS, 128))
     product_buf[...] = jnp.zeros_like(product_buf)
-    rank_of_row = iota((ROWS, WIDTH), 0) // (LAYERS * STEPS)
-    for i in range(REQ):
-        q, rank = lax.shift_right_logical(slots_ref[i], 1), slots_ref[i] & 1
-        state = jnp.concatenate([states_ref[i * LAYERS + l] for l in range(LAYERS)], axis=1)
-        prod = lax.dot_general(
-            read_buf[q], state, (((1,), (1,)), ((), ())), preferred_element_type=F32
-        )
-        prod = prod[0:ROWS] + prod[ROWS:]
-        product_buf[q] = product_buf[q] + jnp.where(rank_of_row == rank, prod, 0.0)
     row, lane = iota((ROWS, 128), 0), iota((ROWS, 128), 1)
     mine = lane // 2 == row
     spread = one_hot(
         (iota((128, 128), 0) % 2 == iota((128, 128), 1) // HEAD_DIM) & (iota((128, 128), 0) < 16)
     )
-    for t in range(TP):
+
+    def rest(t, q):
         lanes = slice(t * RANK_WIDTH, (t + 1) * RANK_WIDTH)
-        at = ROWS + (2 * t + 2) % ROWS
+        at = (2 * t + 2) % ROWS
         tap2, tap3 = taps_ref[0, :, lanes][None], taps_ref[1, :, lanes][None]
-        shift = params_ref[0, :, lanes][None]
-        decay = params_ref[1, :, lanes][None]
-        skip = params_ref[2, :, lanes][None]
-        for q in range(0, REPLICAS, group):
-            raw = got_ref[q : q + group, t, ROWS : 2 * ROWS, :].astype(F32)[
-                :, at - ROWS : at - ROWS + 1, :
-            ]
-            raw = jnp.where(mine[None], raw, 0.0).astype(BF16).reshape(group * ROWS, 128)
-            rate = dot(raw, spread).reshape(group, ROWS, 128) + shift
-            dt = jnp.maximum(rate, 0.0) + jnp.log1p(jnp.exp(-jnp.abs(rate)))
-            damp = jnp.exp(-dt * decay)
-            fresh = got_ref[q : q + group, t, 0:ROWS, :].astype(F32)
-            x = part_ref[q : q + group, :, lanes]
-            x = x + tap2 * pltpu.roll(fresh, 1, 1) + tap3 * fresh
-            x = x * jax.nn.sigmoid(x)
-            taken = dt * x
-            before = jnp.where(later, pltpu.roll(damp, 1, 1), 1.0)
-            carried = jnp.where(later, pltpu.roll(taken, 1, 1) * dots_buf[1, q : q + group], 0.0)
-            y = damp * (before * product_buf[q : q + group, :, lanes] + carried)
-            y = y + taken * dots_buf[0, q : q + group] + skip * x
+        raw = got_ref[q : q + group, t, ROWS : 2 * ROWS, :].astype(F32)[:, at : at + 1, :]
+        raw = jnp.where(mine[None], raw, 0.0).astype(BF16).reshape(group * ROWS, 128)
+        rate = dot(raw, spread).reshape(group, ROWS, 128) + params_ref[0, :, lanes][None]
+        dt = jnp.maximum(rate, 0.0) + jnp.log1p(jnp.exp(-jnp.abs(rate)))
+        damp = jnp.exp(-dt * params_ref[1, :, lanes][None])
+        fresh = got_ref[q : q + group, t, 0:ROWS, :].astype(F32)
+        x = part_ref[q : q + group, :, lanes]
+        x = x + tap2 * pltpu.roll(fresh, 1, 1) + tap3 * fresh
+        x = x * jax.nn.sigmoid(x)
+        taken = dt * x
+        before = jnp.where(later, pltpu.roll(damp, 1, 1), 1.0)
+        carried = jnp.where(later, pltpu.roll(taken, 1, 1) * dots_buf[1, q : q + group], 0.0)
+        gain_buf[q : q + group, :, lanes] = damp * before
+        base_buf[q : q + group, :, lanes] = (
+            damp * carried + taken * dots_buf[0, q : q + group] + params_ref[2, :, lanes][None] * x
+        )
+
+    parts = [(t, q) for q in range(0, REPLICAS, group) for t in range(TP)]
+    rank_of_row = iota((ROWS, WIDTH), 0) // (LAYERS * STEPS)
+    for i in range(REQ):
+        q, rank = lax.shift_right_logical(slots_ref[i], 1), slots_ref[i] & 1
+        if i >= NEAR and (i - NEAR) % PIECE == 0:
+            fetch((i - NEAR) // PIECE).wait()
+        state = near_ref if i < NEAR else far_buf
+        at = (i if i < NEAR else i - NEAR) * LAYERS
+        state = jnp.concatenate([state[at + l] for l in range(LAYERS)], axis=1)
+        prod = lax.dot_general(
+            read_buf[q], state, (((1,), (1,)), ((), ())), preferred_element_type=F32
+        )
+        prod = prod[0:ROWS] + prod[ROWS:]
+        product_buf[q] = product_buf[q] + jnp.where(rank_of_row == rank, prod, 0.0)
+        rest(*parts[i])
+    for q in range(0, REPLICAS, group):
+        for t in range(TP):
+            lanes = slice(t * RANK_WIDTH, (t + 1) * RANK_WIDTH)
+            y = base_buf[q : q + group, :, lanes]
+            y = y + gain_buf[q : q + group, :, lanes] * product_buf[q : q + group, :, lanes]
             out_ref[q : q + group, t] = y.astype(BF16)
 
 
@@ -337,7 +368,7 @@
         pack_kernel,
         out_shape=(
             jax.ShapeDtypeStruct((N_REP, N_HEAD, 2 * ROWS, 128), BF16),
-            jax.ShapeDtypeStruct((REQ * LAYERS, WIDTH, STATE), BF16),
+            jax.ShapeDtypeStruct((NEAR * LAYERS, WIDTH, STATE), BF16),
             pltpu.SMEM((REQ,), jnp.int32),
             jax.ShapeDtypeStruct((REPLICAS, ROWS, WIDTH + 2 * STATE), F32),
             jax.ShapeDtypeStruct((2, ROWS, WIDTH + 2 * STATE), F32),
@@ -397,16 +428,20 @@
     decoded = pl.pallas_call(
         step_kernel,
         out_shape=jax.ShapeDtypeStruct((REPLICAS, TP, ROWS, 128), BF16),
-        in_specs=[VMEM, VMEM, SMEM, VMEM, VMEM, VMEM],
+        in_specs=[VMEM, VMEM, HBM, SMEM, VMEM, VMEM, VMEM],
         out_specs=VMEM,
         scratch_shapes=[
             pltpu.VMEM((REPLICAS, 2 * ROWS, LAYERS * STATE), BF16),
             pltpu.VMEM((2, REPLICAS, ROWS, 128), F32),
             pltpu.VMEM((REPLICAS, ROWS, WIDTH), F32),
+            pltpu.VMEM((REPLICAS, ROWS, WIDTH), F32),
+            pltpu.VMEM((REPLICAS, ROWS, WIDTH), F32),
+            pltpu.VMEM((max(FAR, 1) * LAYERS, WIDTH, STATE), BF16),
+            pltpu.SemaphoreType.DMA((FAR // PIECE,)),
         ],
         compiler_params=pltpu.CompilerParams(vmem_limit_bytes=20 << 20),
         name="step",
-    )(got, near, slots, part, taps, params)
+    )(got, near, states, slots, part, taps, params)
     back = lax.all_to_all(
         decoded.reshape(REPLICAS * TP, ROWS, 128), AXES, 0, 0, tiled=True
     ).reshape(N_REP, N_HEAD, ROWS, 128)

time: 48.7 us -> 47.3 us (0.971)
  Pallas kernels: 7.77 us -> 6.46 us
    pallas_call x1, Pallas kernels: 3.91 us -> 2.84 us  [shards(): pl.pallas_call(pack_kernel, out_shape=(jax.ShapeDtypeStruct((N_REP, N_HEA...]
where the time goes in v3:
time: 47.3 us; the launch traced here: 47.2 us
  blocking collectives  40.7 us (86%)
  Pallas kernels  6.46 us (14%)
    all_to_all x1, blocking collectives, shards(): lax.all_to_all(packed.reshape(N_REP * N_HEAD, 2 * ROWS, 128), AXES, 0, 0,...  25.4 us
    all_to_all x1, blocking collectives, shards(): lax.all_to_all(decoded.reshape(REPLICAS * TP, ROWS, 128), AXES, 0, 0, til...  15.2 us
    pallas_call x1, Pallas kernels, shards(): pl.pallas_call(step_kernel, out_shape=jax.ShapeDtypeStruct((REPLICAS, TP,...  2.89 us
    pallas_call x1, Pallas kernels, shards(): pl.pallas_call(pack_kernel, out_shape=(jax.ShapeDtypeStruct((N_REP, N_HEA...  2.84 us

profile of v3, /device:TPU:1, one launch (start us, length us, event | category | flops | bytes accessed | tf_op | source)
XLA Modules:
  0.0 47.2 jit_solution(13378686133013023153)
XLA Ops:
  0.0 2.8 %pack.1 = (bf16[8,16,16,128]{3,2,1,0:T(8,128)(2,1)S(1)}, bf16[36,512,128]{2,1,0:T(8,128)(2,1)S(1)}, s32[32]{0:T(128)S(4)}, f32[32,8,768]{2,1,0:T(8,128)S(1)}, f3...) custom-call(bf16[1,1,8,2,2,2,2048]{6,5,4,3,2,1,0:T(2,128)(2,1)} %inner_hbm.1, ...), custom_call_target="tpu_custom_call" | custom-call | tf_op jit(solution)/shard_map/pack/pallas_call | solution.py:367
  2.8 25.4 %all_to_all.10 = bf16[128,16,128]{2,1,0:T(8,128)(2,1)S(1)} all-to-all(bf16[128,16,128]{2,1,0:T(8,128)(2,1)S(1)} %bitcast.11), channel_id=1, replica_groups=mesh['rep'=8,'head'=16] {'rep','head'}, dimensions={0} | all-to-all | bytes 1048576 | tf_op jit(solution)/shard_map/all_to_all | solution.py:425
  28.3 2.9 %step.1 = bf16[32,4,8,128]{3,2,1,0:T(8,128)(2,1)S(1)} custom-call(bf16[32,4,16,128]{3,2,1,0:T(8,128)(2,1)S(1)} %bitcast.8, bf16[36,512,128]{2,1,0:T(8,128)(2,1)S(1)} %get-tuple-element.12.near_ref, bf16[64,512,128]{2,1,0:T(8,128)(2,1)} %bitcast.13, s32[32]{0:T(128)S(4)} %get-tuple-element.13.slots_ref, f32[32,8,768]{2,1,0:T(8,128)S(1)} %get-tuple-element.14.part_ref, ...), custom_call_target="tpu_custom_call" | custom-call | tf_op jit(solution)/shard_map/step/pallas_call | solution.py:428
  31.2 15.2 %all_to_all.11 = bf16[128,8,128]{2,1,0:T(8,128)(2,1)S(1)} all-to-all(bf16[128,8,128]{2,1,0:T(8,128)(2,1)S(1)} %bitcast.9), channel_id=1, replica_groups=mesh['rep'=8,'head'=16] {'rep','head'}, dimensions={0} | all-to-all | bytes 524288 | tf_op jit(solution)/shard_map/all_to_all | solution.py:445
  46.4 0.7 %unpack.1 = bf16[1,1,8,2,2,2,2048]{6,5,4,3,2,1,0:T(2,128)(2,1)} custom-call(bf16[8,16,8,128]{3,2,1,0:T(8,128)(2,1)S(1)} %bitcast.10), custom_call_target="tpu_custom_call" | custom-call | tf_op jit(solution)/shard_map/unpack/pallas_call | solution.py:448

commit v4 on v3

--- a/solution.py
+++ b/solution.py
@@ -19,6 +19,7 @@
 RANK_WIDTH = WIDTH // TP
 GROUP_SPAN = 1024
 ROWS = CAP * LAYERS * STEPS
+PAIRS = CAP * LAYERS + 3
 SLOT_ROWS = REPLICAS * ROWS
 FAR = 14
 NEAR = REQ - FAR
@@ -132,7 +133,6 @@
     def _(q):
         counts[q] = 0
 
-    turn = (iota((ROWS, 128), 0) - 2 * rank) & 7
     copies[0].wait()
     for r in range(N_REP):
         rate_buf[r * ROWS : (r + 1) * ROWS] = jnp.concatenate(
@@ -154,21 +154,17 @@
     copies[1].wait()
     copies[2].wait()
     for r in range(N_REP):
-        inner = jnp.concatenate(
-            [inner_buf[r, c, l].astype(F32) for c in range(CAP) for l in range(LAYERS)], axis=0
-        ).astype(BF16)
-        fresh = group_buf[r].astype(F32)
+        fresh = group_buf[r]
+        inner = [inner_buf[r, c, l] for c in range(CAP) for l in range(LAYERS)]
         for h in range(N_HEAD):
-            out_ref[r, h, 0:ROWS, :] = inner[:, h * 128 : (h + 1) * 128]
+            for m in range(CAP * LAYERS):
+                out_ref[r, h, m] = inner[m][:, h * 128 : (h + 1) * 128]
             at = (h // 2) * 128
-            b_new = fresh[:, at : at + 128]
-            c_new = fresh[:, GROUP_SPAN + at : GROUP_SPAN + at + 128]
-            tile = jnp.where(turn == 0, b_new[0:1], 0.0)
-            tile = jnp.where(turn == 1, b_new[1:2], tile)
-            tile = jnp.where(turn == 4, c_new[0:1], tile)
-            tile = jnp.where(turn == 5, c_new[1:2], tile)
-            tile = jnp.where(turn == 2, rate_rows[h : h + 1, r * 128 : (r + 1) * 128], tile)
-            out_ref[r, h, ROWS : 2 * ROWS, :] = tile.astype(BF16)
+            out_ref[r, h, 4] = fresh[:, at : at + 128]
+            out_ref[r, h, 5] = fresh[:, GROUP_SPAN + at : GROUP_SPAN + at + 128]
+            out_ref[r, h, 6] = jnp.broadcast_to(
+                rate_rows[h : h + 1, r * 128 : (r + 1) * 128], (2, 128)
+            ).astype(BF16)
     for copy in tails:
         copy.wait()
     for i in range(REQ):
@@ -254,7 +250,6 @@
     def _(n):
         fetch(n).start()
 
-    pair = iota((1, ROWS, 128), 1) // 2
     later = iota((1, ROWS, 128), 1) % 2 == 1
     layer = (iota((1, 2 * ROWS, 128), 1) // STEPS) % LAYERS
     tap2_b = taps_ref[0, :, WIDTH : WIDTH + STATE][None]
@@ -263,12 +258,10 @@
     tap3_c = taps_ref[1, :, WIDTH + STATE :][None]
     group = 4
     for q in range(0, REPLICAS, group):
-        tiles = [got_ref[q : q + group, t, ROWS : 2 * ROWS, :].astype(F32) for t in range(TP)]
-        b_new, c_new = tiles[0], tiles[2]
-        for t in range(1, TP):
-            b_new = jnp.where(pair == t, tiles[t], b_new)
-            c_new = jnp.where(pair == t, tiles[(t + 2) % TP], c_new)
-        c_new = pltpu.roll(c_new, 4, 1)
+        b_new, c_new = [
+            jnp.concatenate([got_ref[q : q + group, t, m].astype(F32) for t in range(TP)], axis=1)
+            for m in (4, 5)
+        ]
         b_act = part_ref[q : q + group, :, WIDTH : WIDTH + STATE]
         c_act = part_ref[q : q + group, :, WIDTH + STATE :]
         b_act = b_act + tap2_b * pltpu.roll(b_new, 1, 1) + tap3_b * b_new
@@ -292,14 +285,15 @@
 
     def rest(t, q):
         lanes = slice(t * RANK_WIDTH, (t + 1) * RANK_WIDTH)
-        at = (2 * t + 2) % ROWS
         tap2, tap3 = taps_ref[0, :, lanes][None], taps_ref[1, :, lanes][None]
-        raw = got_ref[q : q + group, t, ROWS : 2 * ROWS, :].astype(F32)[:, at : at + 1, :]
+        raw = got_ref[q : q + group, t, 6].astype(F32)[:, 0:1, :]
         raw = jnp.where(mine[None], raw, 0.0).astype(BF16).reshape(group * ROWS, 128)
         rate = dot(raw, spread).reshape(group, ROWS, 128) + params_ref[0, :, lanes][None]
         dt = jnp.maximum(rate, 0.0) + jnp.log1p(jnp.exp(-jnp.abs(rate)))
         damp = jnp.exp(-dt * params_ref[1, :, lanes][None])
-        fresh = got_ref[q : q + group, t, 0:ROWS, :].astype(F32)
+        fresh = jnp.concatenate(
+            [got_ref[q : q + group, t, m].astype(F32) for m in range(CAP * LAYERS)], axis=1
+        )
         x = part_ref[q : q + group, :, lanes]
         x = x + tap2 * pltpu.roll(fresh, 1, 1) + tap3 * fresh
         x = x * jax.nn.sigmoid(x)
@@ -367,7 +361,7 @@
     packed, near, slots, part, taps, params = pl.pallas_call(
         pack_kernel,
         out_shape=(
-            jax.ShapeDtypeStruct((N_REP, N_HEAD, 2 * ROWS, 128), BF16),
+            jax.ShapeDtypeStruct((N_REP, N_HEAD, PAIRS, 2, 128), BF16),
             jax.ShapeDtypeStruct((NEAR * LAYERS, WIDTH, STATE), BF16),
             pltpu.SMEM((REQ,), jnp.int32),
             jax.ShapeDtypeStruct((REPLICAS, ROWS, WIDTH + 2 * STATE), F32),
@@ -423,8 +417,8 @@
         ]
     )
     got = lax.all_to_all(
-        packed.reshape(N_REP * N_HEAD, 2 * ROWS, 128), AXES, 0, 0, tiled=True
-    ).reshape(REPLICAS, TP, 2 * ROWS, 128)
+        packed.reshape(N_REP * N_HEAD, PAIRS, 2, 128), AXES, 0, 0, tiled=True
+    ).reshape(REPLICAS, TP, PAIRS, 2, 128)
     decoded = pl.pallas_call(
         step_kernel,
         out_shape=jax.ShapeDtypeStruct((REPLICAS, TP, ROWS, 128), BF16),

time: 47.3 us -> 46.7 us (0.987)
  blocking collectives: 40.7 us -> 40 us
    all_to_all x1, blocking collectives: 25.4 us -> 24.8 us  [shards(): lax.all_to_all(packed.reshape(N_REP * N_HEAD, PAIRS, 2, 128), AXES, 0, 0,...]
where the time goes in v4:
time: 46.7 us; the launch traced here: 46.5 us
  blocking collectives  40 us (86%)
  Pallas kernels  6.49 us (14%)
    all_to_all x1, blocking collectives, shards(): lax.all_to_all(packed.reshape(N_REP * N_HEAD, PAIRS, 2, 128), AXES, 0, 0,...  24.8 us
    all_to_all x1, blocking collectives, shards(): lax.all_to_all(decoded.reshape(REPLICAS * TP, ROWS, 128), AXES, 0, 0, til...  15.3 us
    pallas_call x1, Pallas kernels, shards(): pl.pallas_call(step_kernel, out_shape=jax.ShapeDtypeStruct((REPLICAS, TP,...  2.91 us
    pallas_call x1, Pallas kernels, shards(): pl.pallas_call(pack_kernel, out_shape=(jax.ShapeDtypeStruct((N_REP, N_HEA...  2.84 us

profile of v4, /device:TPU:1, one launch (start us, length us, event | category | flops | bytes accessed | tf_op | source)
XLA Modules:
  0.0 46.5 jit_solution(1967425085735153053)
XLA Ops:
  0.0 2.8 %pack.1 = (bf16[8,16,7,2,128]{4,3,2,1,0:T(2,128)(2,1)S(1)}, bf16[36,512,128]{2,1,0:T(8,128)(2,1)S(1)}, s32[32]{0:T(128)S(4)}, f32[32,8,768]{2,1,0:T(8,128)S(1)},...) custom-call(bf16[1,1,8,2,2,2,2048]{6,5,4,3,2,1,0:T(2,128)(2,1)} %inner_hbm.1, ...), custom_call_target="tpu_custom_call" | custom-call | tf_op jit(solution)/shard_map/pack/pallas_call | solution.py:361
  2.8 24.8 %all_to_all.10 = bf16[128,7,2,128]{3,2,1,0:T(2,128)(2,1)S(1)} all-to-all(bf16[128,7,2,128]{3,2,1,0:T(2,128)(2,1)S(1)} %bitcast.11), channel_id=1, replica_groups=mesh['rep'=8,'head'=16] {'rep','head'}, dimensions={0} | all-to-all | bytes 917504 | tf_op jit(solution)/shard_map/all_to_all | solution.py:419
  27.6 2.9 %step.1 = bf16[32,4,8,128]{3,2,1,0:T(8,128)(2,1)S(1)} custom-call(bf16[32,4,7,2,128]{4,3,2,1,0:T(2,128)(2,1)S(1)} %bitcast.8, bf16[36,512,128]{2,1,0:T(8,128)(2,1)S(1)} %get-tuple-element.12.near_ref, bf16[64,512,128]{2,1,0:T(8,128)(2,1)} %bitcast.13, s32[32]{0:T(128)S(4)} %get-tuple-element.13.slots_ref, f32[32,8,768]{2,1,0:T(8,128)S(1)} %get-tuple-element.14.part_ref, ...), custom_call_target="tpu_custom_call" | custom-call | tf_op jit(solution)/shard_map/step/pallas_call | solution.py:422
  30.5 15.3 %all_to_all.11 = bf16[128,8,128]{2,1,0:T(8,128)(2,1)S(1)} all-to-all(bf16[128,8,128]{2,1,0:T(8,128)(2,1)S(1)} %bitcast.9), channel_id=1, replica_groups=mesh['rep'=8,'head'=16] {'rep','head'}, dimensions={0} | all-to-all | bytes 524288 | tf_op jit(solution)/shard_map/all_to_all | solution.py:439
  45.8 0.7 %unpack.1 = bf16[1,1,8,2,2,2,2048]{6,5,4,3,2,1,0:T(2,128)(2,1)} custom-call(bf16[8,16,8,128]{3,2,1,0:T(8,128)(2,1)S(1)} %bitcast.10), custom_call_target="tpu_custom_call" | custom-call | tf_op jit(solution)/shard_map/unpack/pallas_call | solution.py:442

commit v5 on v4

--- a/solution.py
+++ b/solution.py
@@ -7,7 +7,7 @@
 
 F32 = jnp.float32
 BF16 = jnp.bfloat16
-AXES = ("rep", "head")
+AXES = ("head", "rep")
 N_REP, N_HEAD, TP, CAP, LAYERS, STEPS, KERNEL = 8, 16, 4, 2, 2, 2, 4
 SUBS = N_HEAD // TP
 REPLICAS = N_REP * SUBS
@@ -158,11 +158,11 @@
         inner = [inner_buf[r, c, l] for c in range(CAP) for l in range(LAYERS)]
         for h in range(N_HEAD):
             for m in range(CAP * LAYERS):
-                out_ref[r, h, m] = inner[m][:, h * 128 : (h + 1) * 128]
+                out_ref[h, r, m] = inner[m][:, h * 128 : (h + 1) * 128]
             at = (h // 2) * 128
-            out_ref[r, h, 4] = fresh[:, at : at + 128]
-            out_ref[r, h, 5] = fresh[:, GROUP_SPAN + at : GROUP_SPAN + at + 128]
-            out_ref[r, h, 6] = jnp.broadcast_to(
+            out_ref[h, r, 4] = fresh[:, at : at + 128]
+            out_ref[h, r, 5] = fresh[:, GROUP_SPAN + at : GROUP_SPAN + at + 128]
+            out_ref[h, r, 6] = jnp.broadcast_to(
                 rate_rows[h : h + 1, r * 128 : (r + 1) * 128], (2, 128)
             ).astype(BF16)
     for copy in tails:
@@ -259,7 +259,7 @@
     group = 4
     for q in range(0, REPLICAS, group):
         b_new, c_new = [
-            jnp.concatenate([got_ref[q : q + group, t, m].astype(F32) for t in range(TP)], axis=1)
+            jnp.concatenate([got_ref[:, t, q // SUBS, m].astype(F32) for t in range(TP)], axis=1)
             for m in (4, 5)
         ]
         b_act = part_ref[q : q + group, :, WIDTH : WIDTH + STATE]
@@ -286,13 +286,13 @@
     def rest(t, q):
         lanes = slice(t * RANK_WIDTH, (t + 1) * RANK_WIDTH)
         tap2, tap3 = taps_ref[0, :, lanes][None], taps_ref[1, :, lanes][None]
-        raw = got_ref[q : q + group, t, 6].astype(F32)[:, 0:1, :]
+        raw = got_ref[:, t, q // SUBS, 6].astype(F32)[:, 0:1, :]
         raw = jnp.where(mine[None], raw, 0.0).astype(BF16).reshape(group * ROWS, 128)
         rate = dot(raw, spread).reshape(group, ROWS, 128) + params_ref[0, :, lanes][None]
         dt = jnp.maximum(rate, 0.0) + jnp.log1p(jnp.exp(-jnp.abs(rate)))
         damp = jnp.exp(-dt * params_ref[1, :, lanes][None])
         fresh = jnp.concatenate(
-            [got_ref[q : q + group, t, m].astype(F32) for m in range(CAP * LAYERS)], axis=1
+            [got_ref[:, t, q // SUBS, m].astype(F32) for m in range(CAP * LAYERS)], axis=1
         )
         x = part_ref[q : q + group, :, lanes]
         x = x + tap2 * pltpu.roll(fresh, 1, 1) + tap3 * fresh
@@ -325,12 +325,12 @@
             lanes = slice(t * RANK_WIDTH, (t + 1) * RANK_WIDTH)
             y = base_buf[q : q + group, :, lanes]
             y = y + gain_buf[q : q + group, :, lanes] * product_buf[q : q + group, :, lanes]
-            out_ref[q : q + group, t] = y.astype(BF16)
+            out_ref[:, t, q // SUBS] = y.astype(BF16)
 
 
 def unpack_kernel(got_ref, out_ref):
     for r in range(N_REP):
-        rows = jnp.concatenate([got_ref[r, h].astype(F32) for h in range(N_HEAD)], axis=1)
+        rows = jnp.concatenate([got_ref[h, r].astype(F32) for h in range(N_HEAD)], axis=1)
         for c in range(CAP):
             for l in range(LAYERS):
                 at = (c * LAYERS + l) * STEPS
@@ -361,7 +361,7 @@
     packed, near, slots, part, taps, params = pl.pallas_call(
         pack_kernel,
         out_shape=(
-            jax.ShapeDtypeStruct((N_REP, N_HEAD, PAIRS, 2, 128), BF16),
+            jax.ShapeDtypeStruct((N_HEAD, N_REP, PAIRS, 2, 128), BF16),
             jax.ShapeDtypeStruct((NEAR * LAYERS, WIDTH, STATE), BF16),
             pltpu.SMEM((REQ,), jnp.int32),
             jax.ShapeDtypeStruct((REPLICAS, ROWS, WIDTH + 2 * STATE), F32),
@@ -417,11 +417,11 @@
         ]
     )
     got = lax.all_to_all(
-        packed.reshape(N_REP * N_HEAD, PAIRS, 2, 128), AXES, 0, 0, tiled=True
-    ).reshape(REPLICAS, TP, PAIRS, 2, 128)
+        packed.reshape(N_HEAD * N_REP, PAIRS, 2, 128), AXES, 0, 0, tiled=True
+    ).reshape(SUBS, TP, N_REP, PAIRS, 2, 128)
     decoded = pl.pallas_call(
         step_kernel,
-        out_shape=jax.ShapeDtypeStruct((REPLICAS, TP, ROWS, 128), BF16),
+        out_shape=jax.ShapeDtypeStruct((SUBS, TP, N_REP, ROWS, 128), BF16),
         in_specs=[VMEM, VMEM, HBM, SMEM, VMEM, VMEM, VMEM],
         out_specs=VMEM,
         scratch_shapes=[
@@ -437,8 +437,8 @@
         name="step",
     )(got, near, states, slots, part, taps, params)
     back = lax.all_to_all(
-        decoded.reshape(REPLICAS * TP, ROWS, 128), AXES, 0, 0, tiled=True
-    ).reshape(N_REP, N_HEAD, ROWS, 128)
+        decoded.reshape(N_HEAD * N_REP, ROWS, 128), AXES, 0, 0, tiled=True
+    ).reshape(N_HEAD, N_REP, ROWS, 128)
     return pl.pallas_call(
         unpack_kernel,
         out_shape=jax.ShapeDtypeStruct((1, 1, N_REP, CAP, LAYERS, STEPS, N_HEAD * 128), BF16),

time: 46.7 us -> 46.3 us (level)
  no operation moved by 1% of the time
where the time goes in v5:
time: 46.3 us; the launch traced here: 46.2 us
  blocking collectives  39.6 us (86%)
  Pallas kernels  6.52 us (14%)
    all_to_all x1, blocking collectives, shards(): lax.all_to_all(packed.reshape(N_HEAD * N_REP, PAIRS, 2, 128), AXES, 0, 0,...  24.1 us
    all_to_all x1, blocking collectives, shards(): lax.all_to_all(decoded.reshape(N_HEAD * N_REP, ROWS, 128), AXES, 0, 0, ti...  15.5 us
    pallas_call x1, Pallas kernels, shards(): pl.pallas_call(step_kernel, out_shape=jax.ShapeDtypeStruct((SUBS, TP, N_R...  2.93 us
    pallas_call x1, Pallas kernels, shards(): pl.pallas_call(pack_kernel, out_shape=(jax.ShapeDtypeStruct((N_HEAD, N_RE...  2.84 us

profile of v5, /device:TPU:1, one launch (start us, length us, event | category | flops | bytes accessed | tf_op | source)
XLA Modules:
  0.0 46.2 jit_solution(14005998588831538109)
XLA Ops:
  0.0 2.8 %pack.1 = (bf16[16,8,7,2,128]{4,3,2,1,0:T(2,128)(2,1)S(1)}, bf16[36,512,128]{2,1,0:T(8,128)(2,1)S(1)}, s32[32]{0:T(128)S(4)}, f32[32,8,768]{2,1,0:T(8,128)S(1)},...) custom-call(bf16[1,1,8,2,2,2,2048]{6,5,4,3,2,1,0:T(2,128)(2,1)} %inner_hbm.1, ...), custom_call_target="tpu_custom_call" | custom-call | tf_op jit(solution)/shard_map/pack/pallas_call | solution.py:361
  2.8 24.1 %all_to_all.10 = bf16[128,7,2,128]{3,2,1,0:T(2,128)(2,1)S(1)} all-to-all(bf16[128,7,2,128]{3,2,1,0:T(2,128)(2,1)S(1)} %bitcast.11), channel_id=1, replica_groups=mesh['rep'=8,'head'=16] {'head','rep'}, dimensions={0} | all-to-all | bytes 917504 | tf_op jit(solution)/shard_map/all_to_all | solution.py:419
  27.0 2.9 %step.1 = bf16[4,4,8,8,128]{4,3,2,1,0:T(8,128)(2,1)S(1)} custom-call(bf16[4,4,8,7,2,128]{5,4,3,2,1,0:T(2,128)(2,1)S(1)} %bitcast.8, bf16[36,512,128]{2,1,0:T(8,128)(2,1)S(1)} %get-tuple-element.12.near_ref, bf16[64,512,128]{2,1,0:T(8,128)(2,1)} %bitcast.13, s32[32]{0:T(128)S(4)} %get-tuple-element.13.slots_ref, ...), custom_call_target="tpu_custom_call" | custom-call | tf_op jit(solution)/shard_map/step/pallas_call | solution.py:422
  29.9 15.5 %all_to_all.11 = bf16[128,8,128]{2,1,0:T(8,128)(2,1)S(1)} all-to-all(bf16[128,8,128]{2,1,0:T(8,128)(2,1)S(1)} %bitcast.9), channel_id=1, replica_groups=mesh['rep'=8,'head'=16] {'head','rep'}, dimensions={0} | all-to-all | bytes 524288 | tf_op jit(solution)/shard_map/all_to_all | solution.py:439
  45.4 0.8 %unpack.1 = bf16[1,1,8,2,2,2,2048]{6,5,4,3,2,1,0:T(2,128)(2,1)} custom-call(bf16[16,8,8,128]{3,2,1,0:T(8,128)(2,1)S(1)} %bitcast.10), custom_call_target="tpu_custom_call" | custom-call | tf_op jit(solution)/shard_map/unpack/pallas_call | solution.py:442

commit v6 on v5

--- a/solution.py
+++ b/solution.py
@@ -23,7 +23,8 @@
 SLOT_ROWS = REPLICAS * ROWS
 FAR = 14
 NEAR = REQ - FAR
-PIECE = 7
+PIECE = 2
+WAITS = {0: (0, 1, 2, 3), 8: (4, 5, 6)}
 HIST_ROWS = REQ * (KERNEL - 1) * LAYERS
 VMEM = pl.BlockSpec(memory_space=pltpu.VMEM)
 SMEM = pl.BlockSpec(memory_space=pltpu.SMEM)
@@ -309,8 +310,8 @@
     rank_of_row = iota((ROWS, WIDTH), 0) // (LAYERS * STEPS)
     for i in range(REQ):
         q, rank = lax.shift_right_logical(slots_ref[i], 1), slots_ref[i] & 1
-        if i >= NEAR and (i - NEAR) % PIECE == 0:
-            fetch((i - NEAR) // PIECE).wait()
+        for n in WAITS.get(i - NEAR, ()):
+            fetch(n).wait()
         state = near_ref if i < NEAR else far_buf
         at = (i if i < NEAR else i - NEAR) * LAYERS
         state = jnp.concatenate([state[at + l] for l in range(LAYERS)], axis=1)

time: 46.3 us -> 46.4 us (level)
  no operation moved by 1% of the time
where the time goes in v6:
time: 46.4 us; the launch traced here: 46.2 us
  blocking collectives  39.6 us (85%)
  Pallas kernels  6.55 us (14%)
    all_to_all x1, blocking collectives, shards(): lax.all_to_all(packed.reshape(N_HEAD * N_REP, PAIRS, 2, 128), AXES, 0, 0,...  24.1 us
    all_to_all x1, blocking collectives, shards(): lax.all_to_all(decoded.reshape(N_HEAD * N_REP, ROWS, 128), AXES, 0, 0, ti...  15.5 us
    pallas_call x1, Pallas kernels, shards(): pl.pallas_call(step_kernel, out_shape=jax.ShapeDtypeStruct((SUBS, TP, N_R...  2.96 us
    pallas_call x1, Pallas kernels, shards(): pl.pallas_call(pack_kernel, out_shape=(jax.ShapeDtypeStruct((N_HEAD, N_RE...  2.84 us

profile of v6, /device:TPU:1, one launch (start us, length us, event | category | flops | bytes accessed | tf_op | source)
XLA Modules:
  0.0 46.2 jit_solution(6047465969864488294)
XLA Ops:
  0.0 2.8 %pack.1 = (bf16[16,8,7,2,128]{4,3,2,1,0:T(2,128)(2,1)S(1)}, bf16[36,512,128]{2,1,0:T(8,128)(2,1)S(1)}, s32[32]{0:T(128)S(4)}, f32[32,8,768]{2,1,0:T(8,128)S(1)},...) custom-call(bf16[1,1,8,2,2,2,2048]{6,5,4,3,2,1,0:T(2,128)(2,1)} %inner_hbm.1, ...), custom_call_target="tpu_custom_call" | custom-call | tf_op jit(solution)/shard_map/pack/pallas_call | solution.py:362
  2.8 24.1 %all_to_all.10 = bf16[128,7,2,128]{3,2,1,0:T(2,128)(2,1)S(1)} all-to-all(bf16[128,7,2,128]{3,2,1,0:T(2,128)(2,1)S(1)} %bitcast.11), channel_id=1, replica_groups=mesh['rep'=8,'head'=16] {'head','rep'}, dimensions={0} | all-to-all | bytes 917504 | tf_op jit(solution)/shard_map/all_to_all | solution.py:420
  27.0 3.0 %step.1 = bf16[4,4,8,8,128]{4,3,2,1,0:T(8,128)(2,1)S(1)} custom-call(bf16[4,4,8,7,2,128]{5,4,3,2,1,0:T(2,128)(2,1)S(1)} %bitcast.8, bf16[36,512,128]{2,1,0:T(8,128)(2,1)S(1)} %get-tuple-element.12.near_ref, bf16[64,512,128]{2,1,0:T(8,128)(2,1)} %bitcast.13, s32[32]{0:T(128)S(4)} %get-tuple-element.13.slots_ref, ...), custom_call_target="tpu_custom_call" | custom-call | tf_op jit(solution)/shard_map/step/pallas_call | solution.py:423
  29.9 15.5 %all_to_all.11 = bf16[128,8,128]{2,1,0:T(8,128)(2,1)S(1)} all-to-all(bf16[128,8,128]{2,1,0:T(8,128)(2,1)S(1)} %bitcast.9), channel_id=1, replica_groups=mesh['rep'=8,'head'=16] {'head','rep'}, dimensions={0} | all-to-all | bytes 524288 | tf_op jit(solution)/shard_map/all_to_all | solution.py:440
  45.4 0.8 %unpack.1 = bf16[1,1,8,2,2,2,2048]{6,5,4,3,2,1,0:T(2,128)(2,1)} custom-call(bf16[16,8,8,128]{3,2,1,0:T(8,128)(2,1)S(1)} %bitcast.10), custom_call_target="tpu_custom_call" | custom-call | tf_op jit(solution)/shard_map/unpack/pallas_call | solution.py:443
